TPU v7x, 32 devices: a whole 2x2x4 slice. The times are simulated.
32 devices in a mesh: groups: 2 (over y), section: 4 (over z), fsdp: 4 (over x, core).
Axes of the slice: x: 2, y: 2, z: 4, core: 2. Of those that a mesh axis runs over, the one named last changes fastest.
Arguments:
- sent_act: bfloat16 [4, 1024, 4096], P('section', 'groups', 'fsdp'), parts along dimension 1, may hold values from -6 to 6
- sent_grad: bfloat16 [4, 1024, 4096], P('section', 'groups', 'fsdp'), parts along dimension 1, may hold values from -6 to 6
- stash_in: bfloat16 [4, 2, 1024, 4096], P('section', None, 'groups', 'fsdp'), parts along dimension 2, may hold values from -6 to 6
- stash_pre: bfloat16 [4, 2, 1024, 4096], P('section', None, 'groups', 'fsdp'), parts along dimension 2, may hold values from -6 to 6
- layer_weight: bfloat16 [4, 4096, 4096], P('section', None, 'fsdp'), may hold values from -0.125 to 0.125
- layer_bias: float32 [4, 4096], P('section', 'fsdp'), may hold values from -3 to 3
- seg_table: bfloat16 [4784, 4096], P('section', 'fsdp'), may hold values from -6 to 6
- seg_index: int32 [1024, 32], P('groups'), parts along dimension 0, may hold values from 0 to 4783
- seg_amp: float32 [1024, 32], P('groups'), parts along dimension 0, may hold values from -1.2 to 1.2
- field_angle: float32 [1024, 2], P('groups'), parts along dimension 0, may hold values from -1 to 1
- angle_weight: float32 [2, 4096], P(None, 'fsdp'), may hold values from -3 to 3
- target: bfloat16 [1024, 4096], P('groups', 'fsdp'), parts along dimension 0, may hold values from -6 to 6
- sched: int32 [4], P('section'), may hold values from 0 to 1
Outputs:
- fwd_out: bfloat16 [4, 1024, 4096], P('section', 'groups', 'fsdp'), parts along dimension 1
- grad_in: bfloat16 [4, 1024, 4096], P('section', 'groups', 'fsdp'), parts along dimension 1
- grad_w: bfloat16 [4, 8192, 4096], P('section', 'groups', 'fsdp'), parts along dimension 1
- grad_bias: float32 [4, 8192], P('section', ('groups', 'fsdp')), parts along dimension 1
There are 2 independent parts, one for each index of `groups`. A program takes and returns all parts, laid end to end along the dimension named above; an argument that names none is the same for every part. Nothing has to cross between parts.
All inputs are finite; a program needn't handle non-finite values.
Results may differ from a plain program's by a relative error of at most 0.017.
Values may be sent and summed in bfloat16 or wider, within the bound.
No kernel may reach another device: no remote copies, remote signals or barrier semaphores. Data moves between devices by JAX's collectives and lax.ppermute only.
A program may use at most 128 MiB of HBM per device.

v0:
```python
import functools

import jax
import jax.numpy as jnp
from jax import lax
from jax.experimental import pallas as pl
from jax.experimental.pallas import tpu as pltpu
from jax.sharding import PartitionSpec as P

F32 = jnp.float32
BF16 = jnp.bfloat16
LANES = 128
GROUP = 8
CORES = 2
ROW, FIRST, SLOT, LAST, BLOCKS = range(5)


def over(axis, shard, pairs):
    return lax.ppermute(shard, axis, pairs)


def swap_cores(shard):
    count = lax.axis_size("fsdp")
    return over("fsdp", shard, [(i, i ^ 1) for i in range(count)])


def to_chip(shard, by):
    count = lax.axis_size("fsdp")
    return over("fsdp", shard, [(i, (i + CORES * by) % count) for i in range(count)])


def costs(flops, moved):
    return pl.CostEstimate(flops=flops, bytes_accessed=moved, transcendentals=0)


ANYWHERE = pl.BlockSpec(memory_space=pl.ANY)


def params():
    return pltpu.CompilerParams(vmem_limit_bytes=20 << 20)


def lookup_kernel(info, idx, amp, fa, aw, table, out, code, low_part, high, low, spread, split, edge):
    rows = table.shape[0]
    whole = rows // LANES * LANES
    rest = rows - whole
    high_count = spread.shape[1] // LANES
    groups, lanes = idx.shape
    per_sample = lanes // GROUP

    @pl.when(pl.program_id(0) == 0)
    def build():
        local_row = idx[...] - info[ROW]
        inside = (local_row >= 0) & (local_row < rows)
        sample = lax.broadcasted_iota(jnp.int32, idx.shape, 1) // per_sample
        code[...] = jnp.where(inside, (local_row // LANES) * GROUP + sample, -1)
        low_part[...] = local_row % LANES
        high[...] = amp[...].astype(BF16).astype(F32)
        low[...] = amp[...] - high[...]
        row_id = lax.broadcasted_iota(jnp.int32, (high_count * GROUP, lanes), 0)
        lane_id = lax.broadcasted_iota(jnp.int32, (LANES, lanes), 0)

        def one(group, unused):
            here = pl.ds(group, 1)
            matched = code[here, :] == row_id
            left_high = jnp.where(matched, high[here, :], 0.0).astype(BF16)
            left_low = jnp.where(matched, low[here, :], 0.0).astype(BF16)
            right = jnp.where(low_part[here, :] == lane_id, 1.0, 0.0).astype(BF16)
            left = jnp.concatenate([left_high, left_low], axis=0)
            summed = lax.dot_general(left, right, NT, preferred_element_type=F32)
            summed = summed[:high_count * GROUP] + summed[high_count * GROUP:]
            for k in range(high_count):
                spread[pl.ds(pl.multiple_of(group * GROUP, GROUP), GROUP), k * LANES:(k + 1) * LANES] = (
                    summed[k * GROUP:(k + 1) * GROUP, :]
                )
            return unused

        lax.fori_loop(0, groups, one, 0, unroll=8)
        split[...] = spread[...].astype(BF16)

    angular = fa[:, 0:1] * aw[0:1, :] + fa[:, 1:2] * aw[1:2, :]
    total = jnp.where(info[FIRST] == 1, angular, 0.0)
    if whole:
        total += jnp.dot(split[:, :whole], table[:whole, :], preferred_element_type=F32)
    if rest:
        edge[...] = jnp.zeros(edge.shape, BF16)
        edge[:rest, :] = table[whole:, :]
        total += jnp.dot(split[:, whole:], edge[...], preferred_element_type=F32)
    out[...] = total.astype(BF16)


def lookup_sum(table, seg_index, seg_amp, field_angle, angle_weight, info):
    rows, width = table.shape
    samples, active = seg_index.shape
    groups, lanes = samples // GROUP, GROUP * active
    columns = -(-rows // LANES) * LANES
    block = min(width, 256)
    small = pl.BlockSpec((groups, lanes), lambda n, info: (0, 0))
    return pl.pallas_call(
        lookup_kernel,
        grid_spec=pltpu.PrefetchScalarGridSpec(
            num_scalar_prefetch=1,
            grid=(width // block,),
            in_specs=[
                small,
                small,
                pl.BlockSpec((samples, 2), lambda n, info: (0, 0)),
                pl.BlockSpec((2, block), lambda n, info: (0, n)),
                pl.BlockSpec((rows, block), lambda n, info: (0, n)),
            ],
            out_specs=pl.BlockSpec((samples, block), lambda n, info: (0, n)),
            scratch_shapes=[
                pltpu.VMEM((groups, lanes), jnp.int32),
                pltpu.VMEM((groups, lanes), jnp.int32),
                pltpu.VMEM((groups, lanes), F32),
                pltpu.VMEM((groups, lanes), F32),
                pltpu.VMEM((samples, columns), F32),
                pltpu.VMEM((samples, columns), BF16),
                pltpu.VMEM((LANES, block), BF16),
            ],
        ),
        out_shape=jax.ShapeDtypeStruct((samples, width), BF16),
        compiler_params=params(),
        cost_estimate=costs(10 * samples * rows * width, 2 * rows * width),
        name="lookup_sum",
    )(info, seg_index.reshape(groups, lanes), seg_amp.reshape(groups, lanes), field_angle, angle_weight, table)


NT = (((1,), (1,)), ((), ()))


def cuts(rows):
    return [rows // 8 * 3, rows - rows // 8 * 3]


def first_terms_kernel(info, came, pre, target, first, second, after, later, grad, *outs):
    piece = 32

    @pl.when(pl.program_id(0) == 0)
    def differentiate():
        def one(k, unused):
            span = pl.ds(pl.multiple_of(k * piece, piece), piece)
            act, pullback = jax.vjp(jax.nn.gelu, pre[0, 0, span, :].astype(F32))
            slope = pullback(jnp.ones_like(act))[0]
            missed = act - target[span, :].astype(F32)
            cotangent = jnp.where(info[LAST] == 1, missed, came[span, :].astype(F32))
            grad[span, :] = (cotangent * slope).astype(BF16)
            return unused

        lax.fori_loop(0, grad.shape[0] // piece, one, 0)

    cut = outs[0].shape[0]
    for block, (upper, lower) in zip((first, second), (outs[:2], outs[2:])):
        term = lax.dot_general(grad[...], block[...], NT, preferred_element_type=F32).astype(BF16)
        upper[...] = term[:cut]
        lower[...] = term[cut:]


def first_terms(came, stash_pre, target, weight, info, at, after, later):
    rows, width = came.shape
    block = min(width, 256)
    steps = width // block
    pieces = cuts(rows) * 2
    shapes = [jax.ShapeDtypeStruct((piece, width), BF16) for piece in pieces]
    whole = pl.BlockSpec((rows, width), lambda n, info: (0, 0))
    out_specs = [pl.BlockSpec((piece, block), lambda n, info: (0, n)) for piece in pieces]
    return pl.pallas_call(
        first_terms_kernel,
        grid_spec=pltpu.PrefetchScalarGridSpec(
            num_scalar_prefetch=1,
            grid=(steps,),
            in_specs=[
                whole,
                pl.BlockSpec((1, 1, rows, width), lambda n, info: (0, info[SLOT], 0, 0)),
                whole,
                pl.BlockSpec((block, width), lambda n, info: (info[at + 1] * steps + n, 0)),
                pl.BlockSpec((block, width), lambda n, info: (info[at] * steps + n, 0)),
                ANYWHERE,
                ANYWHERE,
            ],
            out_specs=[whole] + out_specs,
        ),
        out_shape=[jax.ShapeDtypeStruct((rows, width), BF16)] + shapes,
        compiler_params=params(),
        cost_estimate=costs(4 * rows * width * width, 4 * width * width + 6 * rows * width),
        name="gradient_terms",
    )(info, came, stash_pre, target, weight, weight, after, later)


def terms_kernel(info, grad, first, second, after, later, first_out, second_out):
    first_out[...] = lax.dot_general(grad[...], first[...], NT, preferred_element_type=F32).astype(BF16)
    second_out[...] = lax.dot_general(grad[...], second[...], NT, preferred_element_type=F32).astype(BF16)


def terms(grad, weight, info, at, after, later):
    rows, width = grad.shape
    block = min(width, 512)
    steps = width // block
    shape = jax.ShapeDtypeStruct((rows, width), BF16)
    out_spec = pl.BlockSpec((rows, block), lambda n, info: (0, n))
    return pl.pallas_call(
        terms_kernel,
        grid_spec=pltpu.PrefetchScalarGridSpec(
            num_scalar_prefetch=1,
            grid=(steps,),
            in_specs=[
                pl.BlockSpec((rows, width), lambda n, info: (0, 0)),
                pl.BlockSpec((block, width), lambda n, info: (info[at + 1] * steps + n, 0)),
                pl.BlockSpec((block, width), lambda n, info: (info[at] * steps + n, 0)),
                ANYWHERE,
                ANYWHERE,
            ],
            out_specs=[out_spec, out_spec],
        ),
        out_shape=[shape, shape],
        compiler_params=params(),
        cost_estimate=costs(0, 0),
        name="input_terms",
    )(info, grad, weight, weight, after, later)


def forward_kernel(finish, count, info, *refs):
    pieces, blocks, carry, out = refs[:count], refs[count:2 * count], refs[2 * count], refs[-1]
    total = carry[...]
    for piece, block in zip(pieces, blocks):
        total += jnp.dot(piece[...], block[...], preferred_element_type=F32)
    if finish:
        total = jax.nn.gelu(total)
    out[...] = total.astype(out.dtype)


def forward_step(pieces, ats, weight, info, carry, rows, h, finish, before):
    half, width = pieces[0].shape
    count = len(pieces)
    block = min(width, 512)
    piece = pl.BlockSpec((half, width), lambda n, info: (0, 0))
    out_rows, place = (rows, h) if finish else (half, 0)
    return pl.pallas_call(
        functools.partial(forward_kernel, finish, count),
        grid_spec=pltpu.PrefetchScalarGridSpec(
            num_scalar_prefetch=1,
            grid=(width // block,),
            in_specs=[piece] * count
            + [pl.BlockSpec((width, block), functools.partial(lambda at, n, info: (info[at], n), at)) for at in ats]
            + [pl.BlockSpec((carry.shape[0], block), lambda n, info: (0, n)), ANYWHERE],
            out_specs=pl.BlockSpec((half, block), lambda n, info: (place, n)),
        ),
        out_shape=jax.ShapeDtypeStruct((out_rows, width), BF16 if finish else F32),
        input_output_aliases={2 * count + 2: 0} if finish and h else {},
        compiler_params=params(),
        cost_estimate=costs(2 * count * half * width * width, 2 * count * width * width + 8 * half * width),
        name="forward_step",
    )(info, *pieces, *[weight] * count, carry, before)


def step_down(shard, stride):
    sections = lax.axis_size("section")
    return over("section", shard, [(s, s - stride) for s in range(stride, sections, 2 * stride)])


def local(
    sent_act,
    sent_grad,
    stash_in,
    stash_pre,
    layer_weight,
    layer_bias,
    seg_table,
    seg_index,
    seg_amp,
    field_angle,
    angle_weight,
    target,
    sched,
):
    section = lax.axis_index("section")
    sections = lax.axis_size("section")
    me = lax.axis_index("fsdp")
    count = lax.axis_size("fsdp")
    chips = count // CORES
    rows = sent_act.shape[1]
    halves = 2
    half = rows // halves
    weight = layer_weight[0]

    numbers = [section * seg_table.shape[0], section == 0, sched[0], section == sections - 1]
    for by in range(chips):
        base = lax.rem(me // CORES + by, chips) * CORES
        core = lax.rem(me, CORES)
        numbers += [base + core, base + 1 - core]
    info = jnp.stack([jnp.asarray(number, jnp.int32) for number in numbers])
    is_first = section == 0
    stashed_in = lax.dynamic_index_in_dim(stash_in[0], sched[0], 0, keepdims=False)
    stashed_full = lax.all_gather(stashed_in, "fsdp", axis=1, tiled=True)

    from_before = over("section", sent_act[0], [(s, s + 1) for s in range(sections - 1)])
    from_next = over("section", sent_grad[0], [(s, s - 1) for s in range(1, sections)])
    rounded = lookup_sum(seg_table, seg_index, seg_amp, field_angle, angle_weight, info)

    received = []
    for by in range(1, chips):
        at = BLOCKS + 2 * by
        if by == 1:
            pre_grad, *terms_out = first_terms(
                from_next, stash_pre, target, weight, info, at, rounded, from_before
            )
            to_other, kept = terms_out[:2], terms_out[2:]
        else:
            to_other, kept = [
                [term[:cuts(rows)[0]], term[cuts(rows)[0]:]]
                for term in terms(pre_grad, weight, info, at, info, info)
            ]
        both = [
            (mine.astype(F32) + swap_cores(other).astype(F32)).astype(BF16)
            for mine, other in zip(kept, to_other)
        ]
        if by == 1:
            token = both[0]
        received.append([to_chip(piece, by) for piece in both])
    grad_bias = jnp.sum(pre_grad.astype(F32), axis=0)

    early = rows // 4 * 3
    near = step_down(rounded[:early], 1)
    near, token = lax.optimization_barrier((near, token))
    late = step_down(rounded[early:], 1)
    leaving = [(rounded[:half].astype(F32) + near[:half].astype(F32)).astype(BF16)]
    grad_w = lax.dot_general(
        stashed_full, pre_grad, (((0,), (0,)), ((), ())), preferred_element_type=F32
    ).astype(BF16)
    late, grad_w, kept_back = lax.optimization_barrier((late, grad_w, leaving[0]))
    late = jnp.concatenate([near[half:], late], axis=0)
    leaving.append((rounded[half:].astype(F32) + late.astype(F32)).astype(BF16))
    stride = 2
    while 2 * stride < sections:
        kept_back = None
        leaving = [(piece.astype(F32) + step_down(piece, stride).astype(F32)).astype(BF16) for piece in leaving]
        stride *= 2
    last = [step_down(leaving[0], stride)]
    last.append(step_down(leaving[1], stride))
    last[0], received[0], grad_w, grad_bias = lax.optimization_barrier(
        (last[0], received[0], grad_w, grad_bias)
    )

    if kept_back is not None:
        leaving[0] = kept_back
    inputs, carries = [], []
    for h in range(halves):
        first_input = (leaving[h].astype(F32) + last[h].astype(F32)).astype(BF16)
        inputs.append(jnp.where(is_first, first_input, from_before[h * half:(h + 1) * half]))
        carry = forward_step(
            [inputs[h], swap_cores(inputs[h])], [BLOCKS, BLOCKS + 1], weight, info, layer_bias, rows, h, False, info
        )
        if h == 0:
            to_other, kept = terms(pre_grad, weight, info, BLOCKS, inputs[0], token)
            last[1], to_other = lax.optimization_barrier((last[1], to_other))
        carries.append(carry)
    beside = kept.astype(F32) + swap_cores(to_other).astype(F32)
    far = [sum(part[h].astype(F32) for part in received) for h in range(2)]
    grad_in = (beside + jnp.concatenate(far, axis=0)).astype(BF16)
    fwd_out = info
    for h, carry in enumerate(carries):
        for by in range(1, chips):
            at = BLOCKS + 2 * by
            finish = by == chips - 1
            arrived = to_chip(inputs[h], chips - by)
            if h:
                arrived, fwd_out, grad_in = lax.optimization_barrier((arrived, fwd_out, grad_in))
                carry = forward_step([arrived], [at], weight, info, carry, rows, h, False, info)
                carry = forward_step(
                    [swap_cores(arrived)], [at + 1], weight, info, carry, rows, h, finish, fwd_out
                )
            else:
                before = carries[-1] if by == 1 else info
                carry = forward_step(
                    [arrived, swap_cores(arrived)], [at, at + 1], weight, info, carry, rows, h, finish, before
                )
        fwd_out = carry
    return (fwd_out[None], grad_in[None], grad_w[None], grad_bias[None])


def solution(mesh):
    return jax.shard_map(
        local,
        mesh=mesh,
        in_specs=(
            P("section", "groups", "fsdp"),
            P("section", "groups", "fsdp"),
            P("section", None, "groups", "fsdp"),
            P("section", None, "groups", "fsdp"),
            P("section", None, "fsdp"),
            P("section", "fsdp"),
            P("section", "fsdp"),
            P("groups", None),
            P("groups", None),
            P("groups", None),
            P(None, "fsdp"),
            P("groups", "fsdp"),
            P("section"),
        ),
        out_specs=(
            P("section", "groups", "fsdp"),
            P("section", "groups", "fsdp"),
            P("section", "groups", "fsdp"),
            P("section", ("groups", "fsdp")),
        ),
        check_vma=False,
    )
```

profile of v0, /device:TPU:0, one launch (start us, length us, event | category | flops | bytes accessed | tf_op | source)
XLA Modules:
  0.0 118.4 jit_solution(10531527913899439747)
XLA Ops:
  11.2 6.6 %collective-permute-start.2 = (bf16[512,1024]{1,0:T(8,128)(2,1)}, bf16[512,1024]{1,0:T(8,128)(2,1)}, u32[]{:S(2)}, u32[]{:S(2)}) collective-permute-start(bf16[512,1024]{1,0:T(8,128)(2,1)} %bitcast.9), channel_id=1, source_target_pairs={{0,4},{4,8},{8,12},{1,5},{5,9},{9,13},{2,6},{6,10},{10,14},{3,7},{... | collective-permute-start | bytes 3145736 | tf_op jit(solution)/shard_map/ppermute | solution.py:19
  18.6 1.9 %copy-done.7 = bf16[1196,1024]{1,0:T(8,128)(2,1)S(1)} copy-done((bf16[1196,1024]{1,0:T(8,128)(2,1)S(1)}, bf16[1196,1024]{1,0:T(8,128)(2,1)}, u32[]{:S(2)}) %copy-start.7) | copy-done | bytes 2449432
  20.5 6.3 %lookup_sum.1.after = bf16[512,1024]{1,0:T(8,128)(2,1)S(1)} custom-call(s32[8]{0:T(128)S(1)} %stack.39.info.refs_5_.refs_3_, s32[64,256]{1,0:T(8,128)S(1)} %reshape.16.idx, f32[64,256]{1,0:T(8,128)S(1)} %reshape.17.amp, f32[512,2]{1,0:T(8,128)S(1)} %copy.23.fa, f32[2,1024]{1,0:T(2,128)S(1)} %copy-done.8, bf16[1196,1024]{1,0:T(8,128)(2,1)S(1)} %copy-done.7), custom_call_target="tpu_custom_call" | custom-call | flops 6270484480 | bytes 2449408 | tf_op jit(solution)/shard_map/lookup_sum/pallas_call | solution.py:99
  28.3 10.8 %collective-permute-done.1.came = bf16[512,1024]{1,0:T(8,128)(2,1)} collective-permute-done((bf16[512,1024]{1,0:T(8,128)(2,1)}, bf16[512,1024]{1,0:T(8,128)(2,1)}, u32[]{:S(2)}, u32[]{:S(2)}) %collective-permute-start.1) | collective-permute-done | bytes 1048608 | tf_op jit(solution)/shard_map/ppermute | solution.py:19
  39.4 3.4 %copy-done.1 = bf16[1,4096,1024]{2,1,0:T(8,128)(2,1)S(1)} copy-done((bf16[1,4096,1024]{2,1,0:T(8,128)(2,1)S(1)}, bf16[1,4096,1024]{2,1,0:T(8,128)(2,1)}, u32[]{:S(2)}) %copy-start.1) | copy-done | bytes 8388632
  42.9 7.0 %gradient_terms.1 = (bf16[512,1024]{1,0:T(8,128)(2,1)S(1)}, bf16[192,1024]{1,0:T(8,128)(2,1)S(1)}, bf16[320,1024]{1,0:T(8,128)(2,1)S(1)}, bf16[192,1024]{1,0:T(8,128)(2,1)S(1)}, bf16[320,1024]{1,0:T(8,128)(2,1)S(1)}) custom-call(s32[8]{0:T(128)S(1)} %stack.39.info.refs_5_.refs_3_, bf16[512,1024]{1,0:T(8,128)(2,1)} %collective-permute-done.1.came, ...), custom_call_target="tpu_custom_call" | custom-call | flops 2147483648 | bytes 7340032 | tf_op jit(solution)/shard_map/gradient_terms/pallas_call | solution.py:167
  52.6 1.6 %collective-permute-start.7 = (bf16[192,1024]{1,0:T(8,128)(2,1)S(1)}, bf16[192,1024]{1,0:T(8,128)(2,1)}, u32[]{:S(2)}, u32[]{:S(2)}) collective-permute-start(bf16[192,1024]{1,0:T(8,128)(2,1)S(1)} %add_convert_fusion.6.later), channel_id=1, source_target_pairs={{0,2},{1,3},{2,0},{3,1},{4,6},{5,7},{6,4},{7,5},{8,10},{9,11},{10,... | collective-permute-start | bytes 1179656 | tf_op jit(solution)/shard_map/ppermute | solution.py:19
  58.5 1.6 %collective-permute-start.9 = (bf16[320,1024]{1,0:T(8,128)(2,1)}, bf16[320,1024]{1,0:T(8,128)(2,1)}, u32[]{:S(2)}, u32[]{:S(2)}) collective-permute-start(bf16[320,1024]{1,0:T(8,128)(2,1)} %add_convert_fusion.1), channel_id=1, source_target_pairs={{0,2},{1,3},{2,0},{3,1},{4,6},{5,7},{6,4},{7,5},{8,10},{9,11},{10,... | collective-permute-start | bytes 1966088 | tf_op jit(solution)/shard_map/ppermute | solution.py:19
  60.2 10.6 %convolution_convert_fusion = bf16[4096,1024]{1,0:T(8,128)(2,1)} fusion(bf16[512,1024]{1,0:T(8,128)(2,1)} %copy-done.2, bf16[1,1,512,4096]{3,2,1,0:T(8,128)(2,1)} %all-gather.3.cloned.1.call-done), kind=kOutput, calls=%fused_computation | convolution fusion | flops 4299161600 | bytes 13631488 | tf_op jit(solution)/shard_map/dot_general | solution.py:327
  70.8 2.2 %collective-permute-done.4 = bf16[128,1024]{1,0:T(8,128)(2,1)} collective-permute-done((bf16[128,1024]{1,0:T(8,128)(2,1)}, bf16[128,1024]{1,0:T(8,128)(2,1)}, u32[]{:S(2)}, u32[]{:S(2)}) %collective-permute-start.4) | collective-permute-done | bytes 262176 | tf_op jit(solution)/shard_map/ppermute | solution.py:19
  76.4 1.5 %collective-permute-done.9 = bf16[320,1024]{1,0:T(8,128)(2,1)} collective-permute-done((bf16[320,1024]{1,0:T(8,128)(2,1)}, bf16[320,1024]{1,0:T(8,128)(2,1)}, u32[]{:S(2)}, u32[]{:S(2)}) %collective-permute-start.9) | collective-permute-done | bytes 655392 | tf_op jit(solution)/shard_map/ppermute | solution.py:19
  77.9 1.6 %fusion.1.after.refs_0_ = bf16[256,1024]{1,0:T(8,128)(2,1)S(1)} fusion(bf16[256,1024]{1,0:T(8,128)(2,1)} %collective-permute-done.6, bf16[256,1024]{1,0:T(8,128)(2,1)} %add_convert_fusion.5, bf16[512,1024]{1,0:T(8,128)(2,1)} %collective-permute-done.2.later, pred[]{:T(512)S(6)} %eq.7), kind=kLoop, calls=%fused_computation.10 | loop fusion | flops 1310720 | bytes 2097153 | tf_op jit(solution)/shard_map/jit(_where)/select_n | solution.py:349
  79.6 1.6 %collective-permute-start.11 = (bf16[256,1024]{1,0:T(8,128)(2,1)S(1)}, bf16[256,1024]{1,0:T(8,128)(2,1)S(1)}, u32[]{:S(2)}, u32[]{:S(2)}) collective-permute-start(bf16[256,1024]{1,0:T(8,128)(2,1)S(1)} %fusion.1.after.refs_0_), channel_id=1, source_target_pairs={{0,2},{1,3},{2,0},{3,1},{4,6},{5,7},{6,4},{7,5},{8,10},{9,11},{10,... | collective-permute-start | bytes 1572872 | tf_op jit(solution)/shard_map/ppermute | solution.py:19
  81.2 3.3 %input_terms.1 = (bf16[512,1024]{1,0:T(8,128)(2,1)S(1)}, bf16[512,1024]{1,0:T(8,128)(2,1)S(1)}) custom-call(s32[8]{0:T(128)S(1)} %stack.39.info.refs_5_.refs_3_, bf16[512,1024]{1,0:T(8,128)(2,1)S(1)} %copy-done.3, bf16[4096,1024]{1,0:T(8,128)(2,1)S(1)} %bitcast.26, bf16[4096,1024]{1,0:T(8,128)(2,1)S(1)} %bitcast.27, ...), custom_call_target="tpu_custom_call" | custom-call | tf_op jit(solution)/shard_map/input_terms/pallas_call | solution.py:201
  84.5 3.6 %collective-permute-done.5 = bf16[256,1024]{1,0:T(8,128)(2,1)S(1)} collective-permute-done((bf16[256,1024]{1,0:T(8,128)(2,1)S(1)}, bf16[256,1024]{1,0:T(8,128)(2,1)S(1)}, u32[]{:S(2)}, u32[]{:S(2)}) %collective-permute-start.5) | collective-permute-done | bytes 524320 | tf_op jit(solution)/shard_map/ppermute | solution.py:19
  90.0 2.7 %collective-permute-done.11.refs_0_ = bf16[256,1024]{1,0:T(8,128)(2,1)S(1)} collective-permute-done((bf16[256,1024]{1,0:T(8,128)(2,1)S(1)}, bf16[256,1024]{1,0:T(8,128)(2,1)S(1)}, u32[]{:S(2)}, u32[]{:S(2)}) %collective-permute-start.11) | collective-permute-done | bytes 524320 | tf_op jit(solution)/shard_map/ppermute | solution.py:19
  92.7 1.6 %collective-permute-start.10 = (bf16[256,1024]{1,0:T(8,128)(2,1)S(1)}, bf16[256,1024]{1,0:T(8,128)(2,1)S(1)}, u32[]{:S(2)}, u32[]{:S(2)}) collective-permute-start(bf16[256,1024]{1,0:T(8,128)(2,1)S(1)} %fusion.2.refs_0_), channel_id=1, source_target_pairs={{0,2},{1,3},{2,0},{3,1},{4,6},{5,7},{6,4},{7,5},{8,10},{9,11},{10,... | collective-permute-start | bytes 1572872 | tf_op jit(solution)/shard_map/ppermute | solution.py:19
  94.3 2.4 %forward_step.5.refs_4_ = f32[256,1024]{1,0:T(8,128)S(1)} custom-call(s32[8]{0:T(128)S(1)} %stack.39.info.refs_5_.refs_3_, bf16[256,1024]{1,0:T(8,128)(2,1)S(1)} %fusion.1.after.refs_0_, bf16[256,1024]{1,0:T(8,128)(2,1)S(1)} %collective-permute-done.13.refs_1_, bf16[4096,1024]{1,0:T(8,128)(2,1)S(1)} %bitcast.28, bf16[4096,1024]{1,0:T(8,128)(2,1)S(1)} %bitcast.29, ...), custom_call_target="tpu_custom_call" | custom-call | flops 1073741824 | bytes 6291456 | tf_op jit(solution)/shard_map/forward_step/pallas_call | solution.py:238
  96.7 2.4 %forward_step.6.refs_5_.refs_2_ = f32[256,1024]{1,0:T(8,128)S(1)} custom-call(s32[8]{0:T(128)S(1)} %stack.39.info.refs_5_.refs_3_, bf16[256,1024]{1,0:T(8,128)(2,1)S(1)} %fusion.2.refs_0_, bf16[256,1024]{1,0:T(8,128)(2,1)S(1)} %collective-permute-done.14.refs_1_, bf16[4096,1024]{1,0:T(8,128)(2,1)S(1)} %bitcast.30, bf16[4096,1024]{1,0:T(8,128)(2,1)S(1)} %bitcast.31, ...), custom_call_target="tpu_custom_call" | custom-call | flops 1073741824 | bytes 6291456 | tf_op jit(solution)/shard_map/forward_step/pallas_call | solution.py:238
  99.1 3.3 %forward_step.7.refs_3_ = bf16[512,1024]{1,0:T(8,128)(2,1)} custom-call(s32[8]{0:T(128)S(1)} %stack.39.info.refs_5_.refs_3_, bf16[256,1024]{1,0:T(8,128)(2,1)S(1)} %collective-permute-done.11.refs_0_, bf16[256,1024]{1,0:T(8,128)(2,1)S(1)} %collective-permute-done.12.refs_1_, bf16[4096,1024]{1,0:T(8,128)(2,1)S(1)} %bitcast.32, ...), custom_call_target="tpu_custom_call" | custom-call | flops 1073741824 | bytes 6291456 | tf_op jit(solution)/shard_map/forward_step/pallas_call | solution.py:238
  102.4 2.8 %add_convert_fusion = bf16[512,1024]{1,0:T(8,128)(2,1)} fusion(bf16[512,1024]{1,0:T(8,128)(2,1)S(1)} %collective-permute-done.15, bf16[512,1024]{1,0:T(8,128)(2,1)S(1)} %get-tuple-element.39, bf16[320,1024]{1,0:T(8,128)(2,1)} %collective-permute-done.9, bf16[192,1024]{1,0:T(8,128)(2,1)} %collective-permute-done.7), kind=kLoop, calls=%fused_computation.2 | loop fusion | flops 4718592 | bytes 4194304 | tf_op jit(solution)/shard_map/convert_element_type | solution.py:359
  105.2 1.8 %collective-permute-done.10.refs_0_ = bf16[256,1024]{1,0:T(8,128)(2,1)S(1)} collective-permute-done((bf16[256,1024]{1,0:T(8,128)(2,1)S(1)}, bf16[256,1024]{1,0:T(8,128)(2,1)S(1)}, u32[]{:S(2)}, u32[]{:S(2)}) %collective-permute-start.10) | collective-permute-done | bytes 524320 | tf_op jit(solution)/shard_map/ppermute | solution.py:19
  107.0 1.8 %forward_step.8.refs_2_ = f32[256,1024]{1,0:T(8,128)S(1)} custom-call(s32[8]{0:T(128)S(1)} %stack.39.info.refs_5_.refs_3_, bf16[256,1024]{1,0:T(8,128)(2,1)S(1)} %collective-permute-done.10.refs_0_, bf16[4096,1024]{1,0:T(8,128)(2,1)S(1)} %bitcast.34, f32[256,1024]{1,0:T(8,128)S(1)} %forward_step.6.refs_5_.refs_2_, s32[8]{0:T(128)S(1)} %stack.39.info.refs_5_.refs_3_), custom_call_target="tpu_custom_call" | custom-call | flops 536870912 | bytes 4194304 | tf_op jit(solution)/shard_map/forward_step/pallas_call | solution.py:238
  109.0 2.6 %forward_step.9 = bf16[512,1024]{1,0:T(8,128)(2,1)} custom-call(s32[8]{0:T(128)S(1)} %stack.39.info.refs_5_.refs_3_, bf16[256,1024]{1,0:T(8,128)(2,1)S(1)} %collective-permute-done.16.refs_0_, bf16[4096,1024]{1,0:T(8,128)(2,1)S(1)} %bitcast.35, f32[256,1024]{1,0:T(8,128)S(1)} %forward_step.8.refs_2_, ...), custom_call_target="tpu_custom_call", output_to_operand_aliasing={{}: (4, {})} | custom-call | flops 536870912 | bytes 4194304 | tf_op jit(solution)/shard_map/forward_step/pallas_call | solution.py:238
  (72 shorter events, 18.1 us)
Async XLA Ops:
  7.2 10.8 %copy-start.11 = (f32[512,32]{0,1:T(8,128)S(1)}, f32[512,32]{0,1:T(8,128)}, u32[]{:S(2)}) copy-start(f32[512,32]{0,1:T(8,128)} %param.21) | copy-start | bytes 196612
  7.2 52.9 %all-gather.3.cloned.1.call-start = ((), (), s32[]{:S(2)}) async-start(), calls=%async_computation | async-start | bytes 5242880 | tf_op jit(solution)/shard_map/all_gather | solution.py:294
  9.8 29.2 %collective-permute-start.1 = (bf16[512,1024]{1,0:T(8,128)(2,1)}, bf16[512,1024]{1,0:T(8,128)(2,1)}, u32[]{:S(2)}, u32[]{:S(2)}) collective-permute-start(bf16[512,1024]{1,0:T(8,128)(2,1)} %bitcast.7), channel_id=1, source_target_pairs={{4,0},{8,4},{12,8},{5,1},{9,5},{13,9},{6,2},{10,6},{14,10},{7,3},{... | collective-permute-start | bytes 3145736 | tf_op jit(solution)/shard_map/ppermute | solution.py:19
  11.2 28.3 %collective-permute-start.2 = (bf16[512,1024]{1,0:T(8,128)(2,1)}, bf16[512,1024]{1,0:T(8,128)(2,1)}, u32[]{:S(2)}, u32[]{:S(2)}) collective-permute-start(bf16[512,1024]{1,0:T(8,128)(2,1)} %bitcast.9), channel_id=1, source_target_pairs={{0,4},{4,8},{8,12},{1,5},{5,9},{9,13},{2,6},{6,10},{10,14},{3,7},{... | collective-permute-start | bytes 3145736 | tf_op jit(solution)/shard_map/ppermute | solution.py:19
  20.5 19.0 %copy-start.4 = (bf16[1,2,512,1024]{3,2,1,0:T(8,128)(2,1)S(1)}, bf16[1,2,512,1024]{3,2,1,0:T(8,128)(2,1)}, u32[]{:S(2)}) copy-start(bf16[1,2,512,1024]{3,2,1,0:T(8,128)(2,1)} %pre.1) | copy-start | bytes 6291460
  26.8 12.6 %copy-start.5 = (bf16[512,1024]{1,0:T(8,128)(2,1)S(1)}, bf16[512,1024]{1,0:T(8,128)(2,1)}, u32[]{:S(2)}) copy-start(bf16[512,1024]{1,0:T(8,128)(2,1)} %target.1) | copy-start | bytes 3145732
  26.9 28.1 %collective-permute-start = (bf16[384,1024]{1,0:T(8,128)(2,1)S(1)}, bf16[384,1024]{1,0:T(8,128)(2,1)S(1)}, u32[]{:S(2)}, u32[]{:S(2)}) collective-permute-start(bf16[384,1024]{1,0:T(8,128)(2,1)S(1)} %slice.33), channel_id=1, source_target_pairs={{4,0},{12,8},{5,1},{13,9},{6,2},{14,10},{7,3},{15,11},{20,16},{28,... | collective-permute-start | bytes 2359304 | tf_op jit(solution)/shard_map/ppermute | solution.py:19
  49.9 2.6 %collective-permute-start.3 = (bf16[192,1024]{1,0:T(8,128)(2,1)S(1)}, bf16[192,1024]{1,0:T(8,128)(2,1)S(1)}, u32[]{:S(2)}, u32[]{:S(2)}) collective-permute-start(bf16[192,1024]{1,0:T(8,128)(2,1)S(1)} %get-tuple-element.27), channel_id=1, source_target_pairs={{0,1},{1,0},{2,3},{3,2},{4,5},{5,4},{6,7},{7,6},{8,9},{9,8},{10,11... | collective-permute-start | bytes 1179656 | tf_op jit(solution)/shard_map/ppermute | solution.py:19
  50.0 7.4 %collective-permute-start.8 = (bf16[320,1024]{1,0:T(8,128)(2,1)S(1)}, bf16[320,1024]{1,0:T(8,128)(2,1)S(1)}, u32[]{:S(2)}, u32[]{:S(2)}) collective-permute-start(bf16[320,1024]{1,0:T(8,128)(2,1)S(1)} %get-tuple-element.33), channel_id=1, source_target_pairs={{0,1},{1,0},{2,3},{3,2},{4,5},{5,4},{6,7},{7,6},{8,9},{9,8},{10,11... | collective-permute-start | bytes 1966088 | tf_op jit(solution)/shard_map/ppermute | solution.py:19
  51.2 21.8 %collective-permute-start.4 = (bf16[128,1024]{1,0:T(8,128)(2,1)}, bf16[128,1024]{1,0:T(8,128)(2,1)}, u32[]{:S(2)}, u32[]{:S(2)}) collective-permute-start(bf16[128,1024]{1,0:T(8,128)(2,1)} %slice.34), channel_id=1, source_target_pairs={{4,0},{12,8},{5,1},{13,9},{6,2},{14,10},{7,3},{15,11},{20,16},{28,... | collective-permute-start | bytes 786440 | tf_op jit(solution)/shard_map/ppermute | solution.py:19
  52.6 23.8 %collective-permute-start.7 = (bf16[192,1024]{1,0:T(8,128)(2,1)S(1)}, bf16[192,1024]{1,0:T(8,128)(2,1)}, u32[]{:S(2)}, u32[]{:S(2)}) collective-permute-start(bf16[192,1024]{1,0:T(8,128)(2,1)S(1)} %add_convert_fusion.6.later), channel_id=1, source_target_pairs={{0,2},{1,3},{2,0},{3,1},{4,6},{5,7},{6,4},{7,5},{8,10},{9,11},{10,... | collective-permute-start | bytes 1179656 | tf_op jit(solution)/shard_map/ppermute | solution.py:19
  56.1 20.3 %collective-permute-start.6 = (bf16[256,1024]{1,0:T(8,128)(2,1)}, bf16[256,1024]{1,0:T(8,128)(2,1)}, u32[]{:S(2)}, u32[]{:S(2)}) collective-permute-start(bf16[256,1024]{1,0:T(8,128)(2,1)} %add_convert_fusion.5), channel_id=1, source_target_pairs={{8,0},{9,1},{10,2},{11,3},{24,16},{25,17},{26,18},{27,19}} | collective-permute-start | bytes 1572872 | tf_op jit(solution)/shard_map/ppermute | solution.py:19
  58.5 19.4 %collective-permute-start.9 = (bf16[320,1024]{1,0:T(8,128)(2,1)}, bf16[320,1024]{1,0:T(8,128)(2,1)}, u32[]{:S(2)}, u32[]{:S(2)}) collective-permute-start(bf16[320,1024]{1,0:T(8,128)(2,1)} %add_convert_fusion.1), channel_id=1, source_target_pairs={{0,2},{1,3},{2,0},{3,1},{4,6},{5,7},{6,4},{7,5},{8,10},{9,11},{10,... | collective-permute-start | bytes 1966088 | tf_op jit(solution)/shard_map/ppermute | solution.py:19
  60.1 21.1 %slice-start = ((s8[8388608]{0:T(1024)(128)(4,1)}), s8[4194304]{0:T(1024)(128)(4,1)S(1)}, s32[]{:S(2)}) async-start(s8[8388608]{0:T(1024)(128)(4,1)} %bitcast.24), calls=%async_computation.1 | async-start | bytes 8388608
  60.2 12.8 %slice-start.2 = ((bf16[384,1024]{1,0:T(8,128)(2,1)}), bf16[128,1024]{1,0:T(8,128)(2,1)S(1)}, s32[]{:S(2)}) async-start(bf16[384,1024]{1,0:T(8,128)(2,1)} %copy-done.9), calls=%async_computation.3 | async-start | bytes 524288 | tf_op jit(solution)/shard_map/slice | solution.py:331
  60.2 21.1 %slice-start.1 = ((s8[8388608]{0:T(1024)(128)(4,1)}), s8[4194304]{0:T(1024)(128)(4,1)S(1)}, s32[]{:S(2)}) async-start(s8[8388608]{0:T(1024)(128)(4,1)} %bitcast.24), calls=%async_computation.2 | async-start | bytes 8388608
  74.1 14.0 %collective-permute-start.5 = (bf16[256,1024]{1,0:T(8,128)(2,1)S(1)}, bf16[256,1024]{1,0:T(8,128)(2,1)S(1)}, u32[]{:S(2)}, u32[]{:S(2)}) collective-permute-start(bf16[256,1024]{1,0:T(8,128)(2,1)S(1)} %add_convert_fusion.4), channel_id=1, source_target_pairs={{8,0},{9,1},{10,2},{11,3},{24,16},{25,17},{26,18},{27,19}} | collective-permute-start | bytes 1572872 | tf_op jit(solution)/shard_map/ppermute | solution.py:19
  79.6 13.1 %collective-permute-start.11 = (bf16[256,1024]{1,0:T(8,128)(2,1)S(1)}, bf16[256,1024]{1,0:T(8,128)(2,1)S(1)}, u32[]{:S(2)}, u32[]{:S(2)}) collective-permute-start(bf16[256,1024]{1,0:T(8,128)(2,1)S(1)} %fusion.1.after.refs_0_), channel_id=1, source_target_pairs={{0,2},{1,3},{2,0},{3,1},{4,6},{5,7},{6,4},{7,5},{8,10},{9,11},{10,... | collective-permute-start | bytes 1572872 | tf_op jit(solution)/shard_map/ppermute | solution.py:19
  88.1 14.2 %collective-permute-start.15 = (bf16[512,1024]{1,0:T(8,128)(2,1)S(1)}, bf16[512,1024]{1,0:T(8,128)(2,1)S(1)}, u32[]{:S(2)}, u32[]{:S(2)}) collective-permute-start(bf16[512,1024]{1,0:T(8,128)(2,1)S(1)} %get-tuple-element.40), channel_id=1, source_target_pairs={{0,1},{1,0},{2,3},{3,2},{4,5},{5,4},{6,7},{7,6},{8,9},{9,8},{10,11... | collective-permute-start | bytes 3145736 | tf_op jit(solution)/shard_map/ppermute | solution.py:19
  88.1 6.1 %collective-permute-start.13 = (bf16[256,1024]{1,0:T(8,128)(2,1)S(1)}, bf16[256,1024]{1,0:T(8,128)(2,1)S(1)}, u32[]{:S(2)}, u32[]{:S(2)}) collective-permute-start(bf16[256,1024]{1,0:T(8,128)(2,1)S(1)} %fusion.1.after.refs_0_), channel_id=1, source_target_pairs={{0,1},{1,0},{2,3},{3,2},{4,5},{5,4},{6,7},{7,6},{8,9},{9,8},{10,11... | collective-permute-start | bytes 1572872 | tf_op jit(solution)/shard_map/ppermute | solution.py:19
  90.0 6.7 %collective-permute-start.14 = (bf16[256,1024]{1,0:T(8,128)(2,1)S(1)}, bf16[256,1024]{1,0:T(8,128)(2,1)S(1)}, u32[]{:S(2)}, u32[]{:S(2)}) collective-permute-start(bf16[256,1024]{1,0:T(8,128)(2,1)S(1)} %fusion.2.refs_0_), channel_id=1, source_target_pairs={{0,1},{1,0},{2,3},{3,2},{4,5},{5,4},{6,7},{7,6},{8,9},{9,8},{10,11... | collective-permute-start | bytes 1572872 | tf_op jit(solution)/shard_map/ppermute | solution.py:19
  92.7 6.4 %collective-permute-start.12 = (bf16[256,1024]{1,0:T(8,128)(2,1)S(1)}, bf16[256,1024]{1,0:T(8,128)(2,1)S(1)}, u32[]{:S(2)}, u32[]{:S(2)}) collective-permute-start(bf16[256,1024]{1,0:T(8,128)(2,1)S(1)} %collective-permute-done.11.refs_0_), channel_id=1, source_target_pairs={{0,1},{1,0},{2,3},{3,2},{4,5},{5,4},{6,7},{7,6},{8,9},{9,8},{10,11... | collective-permute-start | bytes 1572872 | tf_op jit(solution)/shard_map/ppermute | solution.py:19
  92.7 14.3 %collective-permute-start.10 = (bf16[256,1024]{1,0:T(8,128)(2,1)S(1)}, bf16[256,1024]{1,0:T(8,128)(2,1)S(1)}, u32[]{:S(2)}, u32[]{:S(2)}) collective-permute-start(bf16[256,1024]{1,0:T(8,128)(2,1)S(1)} %fusion.2.refs_0_), channel_id=1, source_target_pairs={{0,2},{1,3},{2,0},{3,1},{4,6},{5,7},{6,4},{7,5},{8,10},{9,11},{10,... | collective-permute-start | bytes 1572872 | tf_op jit(solution)/shard_map/ppermute | solution.py:19
  107.0 1.9 %collective-permute-start.16 = (bf16[256,1024]{1,0:T(8,128)(2,1)S(1)}, bf16[256,1024]{1,0:T(8,128)(2,1)S(1)}, u32[]{:S(2)}, u32[]{:S(2)}) collective-permute-start(bf16[256,1024]{1,0:T(8,128)(2,1)S(1)} %collective-permute-done.10.refs_0_), channel_id=1, source_target_pairs={{0,1},{1,0},{2,3},{3,2},{4,5},{5,4},{6,7},{7,6},{8,9},{9,8},{10,11... | collective-permute-start | bytes 1572872 | tf_op jit(solution)/shard_map/ppermute | solution.py:19
  (10 other events, 63.5 us)
Sparse Core Ops, SparseCore 0:
  10.2 37.1 all-gather.2
where the time goes:
time: 121 us; the launch traced here: 118 us
  Pallas kernels  29.1 us (24%)
  waiting for transfers between devices  23.9 us (20%)
  starting transfers between devices  21 us (17%)
  between operations  15.1 us (12%)
  matrix products  10.6 us (9%)
  other arithmetic  9.98 us (8%)
  local copies, waits for them, and re-layouts  8.71 us (7%)
    ppermute x17, waiting for transfers between devices, over(): return lax.ppermute(shard, axis, pairs)  23.9 us
    ppermute x17, starting transfers between devices, over(): return lax.ppermute(shard, axis, pairs)  21 us
    pallas_call x5, Pallas kernels, forward_step(): pl.pallas_call(functools.partial(forward_kernel, finish, count), grid_spe...  12.4 us
    dot_general x1, matrix products, local(): lax.dot_general(stashed_full, pre_grad, (((0,), (0,)), ((), ())), preferr...  10.6 us
    pallas_call x1, Pallas kernels, first_terms(): pl.pallas_call(first_terms_kernel, grid_spec=pltpu.PrefetchScalarGridSpec...  7 us
    unnamed x33, local copies, waits for them, and re-layouts  6.54 us
    pallas_call x1, Pallas kernels, lookup_sum(): pl.pallas_call(lookup_kernel, grid_spec=pltpu.PrefetchScalarGridSpec(num_...  6.33 us
    pallas_call x1, Pallas kernels, terms(): pl.pallas_call(terms_kernel, grid_spec=pltpu.PrefetchScalarGridSpec(num_s...  3.29 us
  transfers between devices with their start and end apart: 18, of which 9 were waited for; matrix products, arithmetic and copies ran while one was open for 19% of the time, Pallas kernels for 22%

commit v1 on v0

--- a/solution.py
+++ b/solution.py
@@ -37,7 +37,7 @@
 
 
 def params():
-    return pltpu.CompilerParams(vmem_limit_bytes=20 << 20)
+    return pltpu.CompilerParams(vmem_limit_bytes=16 << 20)
 
 
 def lookup_kernel(info, idx, amp, fa, aw, table, out, code, low_part, high, low, spread, split, edge):
@@ -133,21 +133,39 @@
     return [rows // 8 * 3, rows - rows // 8 * 3]
 
 
-def first_terms_kernel(info, came, pre, target, first, second, after, later, grad, *outs):
-    piece = 32
-
+def slopes_kernel(info, pre, target, after, slope, closing):
+    act, pullback = jax.vjp(jax.nn.gelu, pre[0, 0].astype(F32))
+    slope[...] = pullback(jnp.ones_like(act))[0]
+    closing[...] = ((act - target[...].astype(F32)) * slope[...]).astype(BF16)
+
+
+def slopes(stash_pre, target, info, after):
+    rows, width = target.shape
+    block = min(rows, 64)
+    span = pl.BlockSpec((block, width), lambda n, info: (n, 0))
+    return pl.pallas_call(
+        slopes_kernel,
+        grid_spec=pltpu.PrefetchScalarGridSpec(
+            num_scalar_prefetch=1,
+            grid=(rows // block,),
+            in_specs=[
+                pl.BlockSpec((1, 1, block, width), lambda n, info: (0, info[SLOT], n, 0)),
+                span,
+                ANYWHERE,
+            ],
+            out_specs=[span, span],
+        ),
+        out_shape=[jax.ShapeDtypeStruct((rows, width), F32), jax.ShapeDtypeStruct((rows, width), BF16)],
+        compiler_params=params(),
+        cost_estimate=costs(0, 10 * rows * width),
+        name="slopes",
+    )(info, stash_pre, target, after)
+
+
+def first_terms_kernel(info, came, slope, closing, first, second, grad, *outs):
     @pl.when(pl.program_id(0) == 0)
     def differentiate():
-        def one(k, unused):
-            span = pl.ds(pl.multiple_of(k * piece, piece), piece)
-            act, pullback = jax.vjp(jax.nn.gelu, pre[0, 0, span, :].astype(F32))
-            slope = pullback(jnp.ones_like(act))[0]
-            missed = act - target[span, :].astype(F32)
-            cotangent = jnp.where(info[LAST] == 1, missed, came[span, :].astype(F32))
-            grad[span, :] = (cotangent * slope).astype(BF16)
-            return unused
-
-        lax.fori_loop(0, grad.shape[0] // piece, one, 0)
+        grad[...] = jnp.where(info[LAST] == 1, closing[...], (came[...].astype(F32) * slope[...]).astype(BF16))
 
     cut = outs[0].shape[0]
     for block, (upper, lower) in zip((first, second), (outs[:2], outs[2:])):
@@ -156,7 +174,7 @@
         lower[...] = term[cut:]
 
 
-def first_terms(came, stash_pre, target, weight, info, at, after, later):
+def first_terms(came, slope, closing, weight, info, at):
     rows, width = came.shape
     block = min(width, 256)
     steps = width // block
@@ -171,12 +189,10 @@
             grid=(steps,),
             in_specs=[
                 whole,
-                pl.BlockSpec((1, 1, rows, width), lambda n, info: (0, info[SLOT], 0, 0)),
+                whole,
                 whole,
                 pl.BlockSpec((block, width), lambda n, info: (info[at + 1] * steps + n, 0)),
                 pl.BlockSpec((block, width), lambda n, info: (info[at] * steps + n, 0)),
-                ANYWHERE,
-                ANYWHERE,
             ],
             out_specs=[whole] + out_specs,
         ),
@@ -184,7 +200,7 @@
         compiler_params=params(),
         cost_estimate=costs(4 * rows * width * width, 4 * width * width + 6 * rows * width),
         name="gradient_terms",
-    )(info, came, stash_pre, target, weight, weight, after, later)
+    )(info, came, slope, closing, weight, weight)
 
 
 def terms_kernel(info, grad, first, second, after, later, first_out, second_out):
@@ -301,9 +317,8 @@
     for by in range(1, chips):
         at = BLOCKS + 2 * by
         if by == 1:
-            pre_grad, *terms_out = first_terms(
-                from_next, stash_pre, target, weight, info, at, rounded, from_before
-            )
+            slope, closing = slopes(stash_pre, target, info, rounded)
+            pre_grad, *terms_out = first_terms(from_next, slope, closing, weight, info, at)
             to_other, kept = terms_out[:2], terms_out[2:]
         else:
             to_other, kept = [
@@ -321,7 +336,7 @@
 
     early = rows // 4 * 3
     near = step_down(rounded[:early], 1)
-    near, token = lax.optimization_barrier((near, token))
+    near, token, from_before = lax.optimization_barrier((near, token, from_before))
     late = step_down(rounded[early:], 1)
     leaving = [(rounded[:half].astype(F32) + near[:half].astype(F32)).astype(BF16)]
     grad_w = lax.dot_general(

time: 121 us -> 118 us (0.975)
  waiting for transfers between devices: 23.9 us -> 19.6 us
  Pallas kernels: 29.1 us -> 30.8 us
    ppermute x17, waiting for transfers between devices: 23.9 us -> 19.5 us  [over(): return lax.ppermute(shard, axis, pairs)]
    pallas_call x0 -> x1, Pallas kernels: none -> 3.4 us  [slopes(): pl.pallas_call(slopes_kernel, grid_spec=pltpu.PrefetchScalarGridSpec(num_...]
    pallas_call x1, Pallas kernels: 7 us -> 5.33 us  [first_terms(): pl.pallas_call(first_terms_kernel, grid_spec=pltpu.PrefetchScalarGridSpec...]
  transfers between devices with their start and end apart: 18 -> 18, of which waited for: 9 -> 7; matrix products, arithmetic and copies ran while one was open for 19% -> 19% of each run, Pallas kernels for 22% -> 24%
where the time goes in v1:
time: 118 us; the launch traced here: 117 us
  Pallas kernels  30.8 us (26%)
  starting transfers between devices  21.6 us (18%)
  waiting for transfers between devices  19.6 us (17%)
  between operations  15.2 us (13%)
  matrix products  10.6 us (9%)
  other arithmetic  10 us (8%)
  local copies, waits for them, and re-layouts  8.73 us (7%)
    ppermute x17, starting transfers between devices, over(): return lax.ppermute(shard, axis, pairs)  21.6 us
    ppermute x17, waiting for transfers between devices, over(): return lax.ppermute(shard, axis, pairs)  19.5 us
    pallas_call x5, Pallas kernels, forward_step(): pl.pallas_call(functools.partial(forward_kernel, finish, count), grid_spe...  12.5 us
    dot_general x1, matrix products, local(): lax.dot_general(stashed_full, pre_grad, (((0,), (0,)), ((), ())), preferr...  10.6 us
    unnamed x33, local copies, waits for them, and re-layouts  6.54 us
    pallas_call x1, Pallas kernels, lookup_sum(): pl.pallas_call(lookup_kernel, grid_spec=pltpu.PrefetchScalarGridSpec(num_...  6.29 us
    pallas_call x1, Pallas kernels, first_terms(): pl.pallas_call(first_terms_kernel, grid_spec=pltpu.PrefetchScalarGridSpec...  5.33 us
    pallas_call x1, Pallas kernels, slopes(): pl.pallas_call(slopes_kernel, grid_spec=pltpu.PrefetchScalarGridSpec(num_...  3.4 us
  transfers between devices with their start and end apart: 18, of which 7 were waited for; matrix products, arithmetic and copies ran while one was open for 19% of the time, Pallas kernels for 24%

profile of v1, /device:TPU:0, one launch (start us, length us, event | category | flops | bytes accessed | tf_op | source)
XLA Modules:
  0.0 116.5 jit_solution(5551454781102465019)
XLA Ops:
  11.2 6.6 %collective-permute-start.3 = (bf16[512,1024]{1,0:T(8,128)(2,1)}, bf16[512,1024]{1,0:T(8,128)(2,1)}, u32[]{:S(2)}, u32[]{:S(2)}) collective-permute-start(bf16[512,1024]{1,0:T(8,128)(2,1)} %bitcast.9), channel_id=1, source_target_pairs={{0,4},{4,8},{8,12},{1,5},{5,9},{9,13},{2,6},{6,10},{10,14},{3,7},{... | collective-permute-start | bytes 3145736 | tf_op jit(solution)/shard_map/ppermute | solution.py:19
  18.5 1.9 %copy-done.7 = bf16[1196,1024]{1,0:T(8,128)(2,1)S(1)} copy-done((bf16[1196,1024]{1,0:T(8,128)(2,1)S(1)}, bf16[1196,1024]{1,0:T(8,128)(2,1)}, u32[]{:S(2)}) %copy-start.7) | copy-done | bytes 2449432
  20.5 6.3 %lookup_sum.1.after = bf16[512,1024]{1,0:T(8,128)(2,1)S(1)} custom-call(s32[8]{0:T(128)S(1)} %stack.39.info.refs_5_.refs_3_, s32[64,256]{1,0:T(8,128)S(1)} %reshape.16.idx, f32[64,256]{1,0:T(8,128)S(1)} %reshape.17.amp, f32[512,2]{1,0:T(8,128)S(1)} %copy.23.fa, f32[2,1024]{1,0:T(2,128)S(1)} %copy-done.8, bf16[1196,1024]{1,0:T(8,128)(2,1)S(1)} %copy-done.7), custom_call_target="tpu_custom_call" | custom-call | flops 6270484480 | bytes 2449408 | tf_op jit(solution)/shard_map/lookup_sum/pallas_call | solution.py:99
  28.3 3.4 %slopes.1 = (f32[512,1024]{1,0:T(8,128)S(1)}, bf16[512,1024]{1,0:T(8,128)(2,1)S(1)}) custom-call(s32[8]{0:T(128)S(1)} %stack.39.info.refs_5_.refs_3_, bf16[1,2,512,1024]{3,2,1,0:T(8,128)(2,1)S(1)} %copy-done.4, bf16[512,1024]{1,0:T(8,128)(2,1)S(1)} %copy-done.5, bf16[512,1024]{1,0:T(8,128)(2,1)S(1)} %lookup_sum.1.after), custom_call_target="tpu_custom_call" | custom-call | bytes 5242880 | tf_op jit(solution)/shard_map/slopes/pallas_call | solution.py:146
  31.7 7.4 %collective-permute-done.1.came = bf16[512,1024]{1,0:T(8,128)(2,1)} collective-permute-done((bf16[512,1024]{1,0:T(8,128)(2,1)}, bf16[512,1024]{1,0:T(8,128)(2,1)}, u32[]{:S(2)}, u32[]{:S(2)}) %collective-permute-start.1) | collective-permute-done | bytes 1048608 | tf_op jit(solution)/shard_map/ppermute | solution.py:19
  39.1 3.4 %copy-done.1 = bf16[1,4096,1024]{2,1,0:T(8,128)(2,1)S(1)} copy-done((bf16[1,4096,1024]{2,1,0:T(8,128)(2,1)S(1)}, bf16[1,4096,1024]{2,1,0:T(8,128)(2,1)}, u32[]{:S(2)}) %copy-start.1) | copy-done | bytes 8388632
  42.5 5.3 %gradient_terms.1 = (bf16[512,1024]{1,0:T(8,128)(2,1)S(1)}, bf16[192,1024]{1,0:T(8,128)(2,1)S(1)}, bf16[320,1024]{1,0:T(8,128)(2,1)S(1)}, bf16[192,1024]{1,0:T(8,128)(2,1)S(1)}, bf16[320,1024]{1,0:T(8,128)(2,1)S(1)}) custom-call(s32[8]{0:T(128)S(1)} %stack.39.info.refs_5_.refs_3_, bf16[512,1024]{1,0:T(8,128)(2,1)} %collective-permute-done.1.came, ...), custom_call_target="tpu_custom_call" | custom-call | flops 2147483648 | bytes 7340032 | tf_op jit(solution)/shard_map/gradient_terms/pallas_call | solution.py:185
  50.6 2.0 %collective-permute-start.7 = (bf16[192,1024]{1,0:T(8,128)(2,1)S(1)}, bf16[192,1024]{1,0:T(8,128)(2,1)}, u32[]{:S(2)}, u32[]{:S(2)}) collective-permute-start(bf16[192,1024]{1,0:T(8,128)(2,1)S(1)} %add_convert_fusion.6.later), channel_id=1, source_target_pairs={{0,2},{1,3},{2,0},{3,1},{4,6},{5,7},{6,4},{7,5},{8,10},{9,11},{10,... | collective-permute-start | bytes 1179656 | tf_op jit(solution)/shard_map/ppermute | solution.py:19
  52.6 3.2 %collective-permute-done = bf16[384,1024]{1,0:T(8,128)(2,1)S(1)} collective-permute-done((bf16[384,1024]{1,0:T(8,128)(2,1)S(1)}, bf16[384,1024]{1,0:T(8,128)(2,1)S(1)}, u32[]{:S(2)}, u32[]{:S(2)}) %collective-permute-start) | collective-permute-done | bytes 786464 | tf_op jit(solution)/shard_map/ppermute | solution.py:19
  59.3 1.5 %collective-permute-start.9 = (bf16[320,1024]{1,0:T(8,128)(2,1)}, bf16[320,1024]{1,0:T(8,128)(2,1)}, u32[]{:S(2)}, u32[]{:S(2)}) collective-permute-start(bf16[320,1024]{1,0:T(8,128)(2,1)} %add_convert_fusion.1), channel_id=1, source_target_pairs={{0,2},{1,3},{2,0},{3,1},{4,6},{5,7},{6,4},{7,5},{8,10},{9,11},{10,... | collective-permute-start | bytes 1966088 | tf_op jit(solution)/shard_map/ppermute | solution.py:19
  60.8 10.6 %convolution_convert_fusion = bf16[4096,1024]{1,0:T(8,128)(2,1)} fusion(bf16[512,1024]{1,0:T(8,128)(2,1)} %copy-done.2, bf16[1,1,512,4096]{3,2,1,0:T(8,128)(2,1)} %all-gather.3.cloned.1.call-done), kind=kOutput, calls=%fused_computation | convolution fusion | flops 4299161600 | bytes 13631488 | tf_op jit(solution)/shard_map/dot_general | solution.py:342
  72.7 1.5 %collective-permute-start.5 = (bf16[256,1024]{1,0:T(8,128)(2,1)S(1)}, bf16[256,1024]{1,0:T(8,128)(2,1)S(1)}, u32[]{:S(2)}, u32[]{:S(2)}) collective-permute-start(bf16[256,1024]{1,0:T(8,128)(2,1)S(1)} %add_convert_fusion.4), channel_id=1, source_target_pairs={{8,0},{9,1},{10,2},{11,3},{24,16},{25,17},{26,18},{27,19}} | collective-permute-start | bytes 1572872 | tf_op jit(solution)/shard_map/ppermute | solution.py:19
  76.1 1.6 %fusion.1.after.refs_0_ = bf16[256,1024]{1,0:T(8,128)(2,1)S(1)} fusion(bf16[256,1024]{1,0:T(8,128)(2,1)} %collective-permute-done.6, bf16[256,1024]{1,0:T(8,128)(2,1)} %add_convert_fusion.5, bf16[512,1024]{1,0:T(8,128)(2,1)} %collective-permute-done.3, pred[]{:T(512)S(6)} %eq.7), kind=kLoop, calls=%fused_computation.10 | loop fusion | flops 1310720 | bytes 2097153 | tf_op jit(solution)/shard_map/jit(_where)/select_n | solution.py:364
  77.7 1.8 %collective-permute-start.11 = (bf16[256,1024]{1,0:T(8,128)(2,1)S(1)}, bf16[256,1024]{1,0:T(8,128)(2,1)S(1)}, u32[]{:S(2)}, u32[]{:S(2)}) collective-permute-start(bf16[256,1024]{1,0:T(8,128)(2,1)S(1)} %fusion.1.after.refs_0_), channel_id=1, source_target_pairs={{0,2},{1,3},{2,0},{3,1},{4,6},{5,7},{6,4},{7,5},{8,10},{9,11},{10,... | collective-permute-start | bytes 1572872 | tf_op jit(solution)/shard_map/ppermute | solution.py:19
  79.6 3.3 %input_terms.1 = (bf16[512,1024]{1,0:T(8,128)(2,1)S(1)}, bf16[512,1024]{1,0:T(8,128)(2,1)S(1)}) custom-call(s32[8]{0:T(128)S(1)} %stack.39.info.refs_5_.refs_3_, bf16[512,1024]{1,0:T(8,128)(2,1)S(1)} %copy-done.3, bf16[4096,1024]{1,0:T(8,128)(2,1)S(1)} %bitcast.26, bf16[4096,1024]{1,0:T(8,128)(2,1)S(1)} %bitcast.27, ...), custom_call_target="tpu_custom_call" | custom-call | tf_op jit(solution)/shard_map/input_terms/pallas_call | solution.py:217
  82.9 5.3 %collective-permute-done.5 = bf16[256,1024]{1,0:T(8,128)(2,1)S(1)} collective-permute-done((bf16[256,1024]{1,0:T(8,128)(2,1)S(1)}, bf16[256,1024]{1,0:T(8,128)(2,1)S(1)}, u32[]{:S(2)}, u32[]{:S(2)}) %collective-permute-start.5) | collective-permute-done | bytes 524320 | tf_op jit(solution)/shard_map/ppermute | solution.py:19
  90.8 1.7 %collective-permute-start.10 = (bf16[256,1024]{1,0:T(8,128)(2,1)S(1)}, bf16[256,1024]{1,0:T(8,128)(2,1)S(1)}, u32[]{:S(2)}, u32[]{:S(2)}) collective-permute-start(bf16[256,1024]{1,0:T(8,128)(2,1)S(1)} %fusion.2.refs_0_), channel_id=1, source_target_pairs={{0,2},{1,3},{2,0},{3,1},{4,6},{5,7},{6,4},{7,5},{8,10},{9,11},{10,... | collective-permute-start | bytes 1572872 | tf_op jit(solution)/shard_map/ppermute | solution.py:19
  92.5 2.4 %forward_step.5.refs_4_ = f32[256,1024]{1,0:T(8,128)S(1)} custom-call(s32[8]{0:T(128)S(1)} %stack.39.info.refs_5_.refs_3_, bf16[256,1024]{1,0:T(8,128)(2,1)S(1)} %fusion.1.after.refs_0_, bf16[256,1024]{1,0:T(8,128)(2,1)S(1)} %collective-permute-done.13.refs_1_, bf16[4096,1024]{1,0:T(8,128)(2,1)S(1)} %bitcast.28, bf16[4096,1024]{1,0:T(8,128)(2,1)S(1)} %bitcast.29, ...), custom_call_target="tpu_custom_call" | custom-call | flops 1073741824 | bytes 6291456 | tf_op jit(solution)/shard_map/forward_step/pallas_call | solution.py:254
  94.9 2.4 %forward_step.6.refs_5_.refs_2_ = f32[256,1024]{1,0:T(8,128)S(1)} custom-call(s32[8]{0:T(128)S(1)} %stack.39.info.refs_5_.refs_3_, bf16[256,1024]{1,0:T(8,128)(2,1)S(1)} %fusion.2.refs_0_, bf16[256,1024]{1,0:T(8,128)(2,1)S(1)} %collective-permute-done.14.refs_1_, bf16[4096,1024]{1,0:T(8,128)(2,1)S(1)} %bitcast.30, bf16[4096,1024]{1,0:T(8,128)(2,1)S(1)} %bitcast.31, ...), custom_call_target="tpu_custom_call" | custom-call | flops 1073741824 | bytes 6291456 | tf_op jit(solution)/shard_map/forward_step/pallas_call | solution.py:254
  97.3 3.4 %forward_step.7.refs_3_ = bf16[512,1024]{1,0:T(8,128)(2,1)} custom-call(s32[8]{0:T(128)S(1)} %stack.39.info.refs_5_.refs_3_, bf16[256,1024]{1,0:T(8,128)(2,1)S(1)} %collective-permute-done.11.refs_0_, bf16[256,1024]{1,0:T(8,128)(2,1)S(1)} %collective-permute-done.12.refs_1_, bf16[4096,1024]{1,0:T(8,128)(2,1)S(1)} %bitcast.32, ...), custom_call_target="tpu_custom_call" | custom-call | flops 1073741824 | bytes 6291456 | tf_op jit(solution)/shard_map/forward_step/pallas_call | solution.py:254
  100.7 2.8 %add_convert_fusion = bf16[512,1024]{1,0:T(8,128)(2,1)} fusion(bf16[512,1024]{1,0:T(8,128)(2,1)S(1)} %collective-permute-done.15, bf16[512,1024]{1,0:T(8,128)(2,1)S(1)} %get-tuple-element.45, bf16[320,1024]{1,0:T(8,128)(2,1)} %collective-permute-done.9, bf16[192,1024]{1,0:T(8,128)(2,1)} %collective-permute-done.7), kind=kLoop, calls=%fused_computation.2 | loop fusion | flops 4718592 | bytes 4194304 | tf_op jit(solution)/shard_map/convert_element_type | solution.py:374
  103.5 1.6 %collective-permute-done.10.refs_0_ = bf16[256,1024]{1,0:T(8,128)(2,1)S(1)} collective-permute-done((bf16[256,1024]{1,0:T(8,128)(2,1)S(1)}, bf16[256,1024]{1,0:T(8,128)(2,1)S(1)}, u32[]{:S(2)}, u32[]{:S(2)}) %collective-permute-start.10) | collective-permute-done | bytes 524320 | tf_op jit(solution)/shard_map/ppermute | solution.py:19
  105.1 1.8 %forward_step.8.refs_2_ = f32[256,1024]{1,0:T(8,128)S(1)} custom-call(s32[8]{0:T(128)S(1)} %stack.39.info.refs_5_.refs_3_, bf16[256,1024]{1,0:T(8,128)(2,1)S(1)} %collective-permute-done.10.refs_0_, bf16[4096,1024]{1,0:T(8,128)(2,1)S(1)} %bitcast.34, f32[256,1024]{1,0:T(8,128)S(1)} %forward_step.6.refs_5_.refs_2_, s32[8]{0:T(128)S(1)} %stack.39.info.refs_5_.refs_3_), custom_call_target="tpu_custom_call" | custom-call | flops 536870912 | bytes 4194304 | tf_op jit(solution)/shard_map/forward_step/pallas_call | solution.py:254
  107.0 2.6 %forward_step.9 = bf16[512,1024]{1,0:T(8,128)(2,1)} custom-call(s32[8]{0:T(128)S(1)} %stack.39.info.refs_5_.refs_3_, bf16[256,1024]{1,0:T(8,128)(2,1)S(1)} %collective-permute-done.16.refs_0_, bf16[4096,1024]{1,0:T(8,128)(2,1)S(1)} %bitcast.35, f32[256,1024]{1,0:T(8,128)S(1)} %forward_step.8.refs_2_, ...), custom_call_target="tpu_custom_call", output_to_operand_aliasing={{}: (4, {})} | custom-call | flops 536870912 | bytes 4194304 | tf_op jit(solution)/shard_map/forward_step/pallas_call | solution.py:254
  (73 shorter events, 17.5 us)
Async XLA Ops:
  7.2 10.6 %copy-start.10 = (s32[512,32]{0,1:T(8,128)S(1)}, s32[512,32]{0,1:T(8,128)}, u32[]{:S(2)}) copy-start(s32[512,32]{0,1:T(8,128)} %param.20) | copy-start | bytes 196612
  7.2 10.8 %copy-start.11 = (f32[512,32]{0,1:T(8,128)S(1)}, f32[512,32]{0,1:T(8,128)}, u32[]{:S(2)}) copy-start(f32[512,32]{0,1:T(8,128)} %param.21) | copy-start | bytes 196612
  7.2 53.6 %all-gather.3.cloned.1.call-start = ((), (), s32[]{:S(2)}) async-start(), calls=%async_computation | async-start | bytes 5242880 | tf_op jit(solution)/shard_map/all_gather | solution.py:310
  9.8 29.2 %collective-permute-start.1 = (bf16[512,1024]{1,0:T(8,128)(2,1)}, bf16[512,1024]{1,0:T(8,128)(2,1)}, u32[]{:S(2)}, u32[]{:S(2)}) collective-permute-start(bf16[512,1024]{1,0:T(8,128)(2,1)} %bitcast.7), channel_id=1, source_target_pairs={{4,0},{8,4},{12,8},{5,1},{9,5},{13,9},{6,2},{10,6},{14,10},{7,3},{... | collective-permute-start | bytes 3145736 | tf_op jit(solution)/shard_map/ppermute | solution.py:19
  11.2 44.7 %collective-permute-start.3 = (bf16[512,1024]{1,0:T(8,128)(2,1)}, bf16[512,1024]{1,0:T(8,128)(2,1)}, u32[]{:S(2)}, u32[]{:S(2)}) collective-permute-start(bf16[512,1024]{1,0:T(8,128)(2,1)} %bitcast.9), channel_id=1, source_target_pairs={{0,4},{4,8},{8,12},{1,5},{5,9},{9,13},{2,6},{6,10},{10,14},{3,7},{... | collective-permute-start | bytes 3145736 | tf_op jit(solution)/shard_map/ppermute | solution.py:19
  26.8 29.0 %collective-permute-start = (bf16[384,1024]{1,0:T(8,128)(2,1)S(1)}, bf16[384,1024]{1,0:T(8,128)(2,1)S(1)}, u32[]{:S(2)}, u32[]{:S(2)}) collective-permute-start(bf16[384,1024]{1,0:T(8,128)(2,1)S(1)} %slice.33), channel_id=1, source_target_pairs={{4,0},{12,8},{5,1},{13,9},{6,2},{14,10},{7,3},{15,11},{20,16},{28,... | collective-permute-start | bytes 2359304 | tf_op jit(solution)/shard_map/ppermute | solution.py:19
  47.8 11.5 %copy-start.2 = (bf16[512,1024]{1,0:T(8,128)(2,1)}, bf16[512,1024]{1,0:T(8,128)(2,1)S(1)}, u32[]{:S(2)}) copy-start(bf16[512,1024]{1,0:T(8,128)(2,1)S(1)} %get-tuple-element.34.grad) | copy-start | bytes 3145732
  47.9 2.6 %collective-permute-start.2 = (bf16[192,1024]{1,0:T(8,128)(2,1)S(1)}, bf16[192,1024]{1,0:T(8,128)(2,1)S(1)}, u32[]{:S(2)}, u32[]{:S(2)}) collective-permute-start(bf16[192,1024]{1,0:T(8,128)(2,1)S(1)} %get-tuple-element.32), channel_id=1, source_target_pairs={{0,1},{1,0},{2,3},{3,2},{4,5},{5,4},{6,7},{7,6},{8,9},{9,8},{10,11... | collective-permute-start | bytes 1179656 | tf_op jit(solution)/shard_map/ppermute | solution.py:19
  47.9 10.3 %collective-permute-start.8 = (bf16[320,1024]{1,0:T(8,128)(2,1)S(1)}, bf16[320,1024]{1,0:T(8,128)(2,1)S(1)}, u32[]{:S(2)}, u32[]{:S(2)}) collective-permute-start(bf16[320,1024]{1,0:T(8,128)(2,1)S(1)} %get-tuple-element.38), channel_id=1, source_target_pairs={{0,1},{1,0},{2,3},{3,2},{4,5},{5,4},{6,7},{7,6},{8,9},{9,8},{10,11... | collective-permute-start | bytes 1966088 | tf_op jit(solution)/shard_map/ppermute | solution.py:19
  49.2 22.3 %collective-permute-start.4 = (bf16[128,1024]{1,0:T(8,128)(2,1)}, bf16[128,1024]{1,0:T(8,128)(2,1)}, u32[]{:S(2)}, u32[]{:S(2)}) collective-permute-start(bf16[128,1024]{1,0:T(8,128)(2,1)} %slice.34), channel_id=1, source_target_pairs={{4,0},{12,8},{5,1},{13,9},{6,2},{14,10},{7,3},{15,11},{20,16},{28,... | collective-permute-start | bytes 786440 | tf_op jit(solution)/shard_map/ppermute | solution.py:19
  50.6 24.4 %collective-permute-start.7 = (bf16[192,1024]{1,0:T(8,128)(2,1)S(1)}, bf16[192,1024]{1,0:T(8,128)(2,1)}, u32[]{:S(2)}, u32[]{:S(2)}) collective-permute-start(bf16[192,1024]{1,0:T(8,128)(2,1)S(1)} %add_convert_fusion.6.later), channel_id=1, source_target_pairs={{0,2},{1,3},{2,0},{3,1},{4,6},{5,7},{6,4},{7,5},{8,10},{9,11},{10,... | collective-permute-start | bytes 1179656 | tf_op jit(solution)/shard_map/ppermute | solution.py:19
  56.9 18.0 %collective-permute-start.6 = (bf16[256,1024]{1,0:T(8,128)(2,1)}, bf16[256,1024]{1,0:T(8,128)(2,1)}, u32[]{:S(2)}, u32[]{:S(2)}) collective-permute-start(bf16[256,1024]{1,0:T(8,128)(2,1)} %add_convert_fusion.5), channel_id=1, source_target_pairs={{8,0},{9,1},{10,2},{11,3},{24,16},{25,17},{26,18},{27,19}} | collective-permute-start | bytes 1572872 | tf_op jit(solution)/shard_map/ppermute | solution.py:19
  59.3 16.8 %collective-permute-start.9 = (bf16[320,1024]{1,0:T(8,128)(2,1)}, bf16[320,1024]{1,0:T(8,128)(2,1)}, u32[]{:S(2)}, u32[]{:S(2)}) collective-permute-start(bf16[320,1024]{1,0:T(8,128)(2,1)} %add_convert_fusion.1), channel_id=1, source_target_pairs={{0,2},{1,3},{2,0},{3,1},{4,6},{5,7},{6,4},{7,5},{8,10},{9,11},{10,... | collective-permute-start | bytes 1966088 | tf_op jit(solution)/shard_map/ppermute | solution.py:19
  60.8 18.7 %slice-start = ((s8[8388608]{0:T(1024)(128)(4,1)}), s8[4194304]{0:T(1024)(128)(4,1)S(1)}, s32[]{:S(2)}) async-start(s8[8388608]{0:T(1024)(128)(4,1)} %bitcast.24), calls=%async_computation.1 | async-start | bytes 8388608
  60.8 10.6 %slice-start.2 = ((bf16[384,1024]{1,0:T(8,128)(2,1)}), bf16[128,1024]{1,0:T(8,128)(2,1)S(1)}, s32[]{:S(2)}) async-start(bf16[384,1024]{1,0:T(8,128)(2,1)} %copy-done.9), calls=%async_computation.3 | async-start | bytes 524288 | tf_op jit(solution)/shard_map/slice | solution.py:346
  60.8 18.7 %slice-start.1 = ((s8[8388608]{0:T(1024)(128)(4,1)}), s8[4194304]{0:T(1024)(128)(4,1)S(1)}, s32[]{:S(2)}) async-start(s8[8388608]{0:T(1024)(128)(4,1)} %bitcast.24), calls=%async_computation.2 | async-start | bytes 8388608
  72.7 15.4 %collective-permute-start.5 = (bf16[256,1024]{1,0:T(8,128)(2,1)S(1)}, bf16[256,1024]{1,0:T(8,128)(2,1)S(1)}, u32[]{:S(2)}, u32[]{:S(2)}) collective-permute-start(bf16[256,1024]{1,0:T(8,128)(2,1)S(1)} %add_convert_fusion.4), channel_id=1, source_target_pairs={{8,0},{9,1},{10,2},{11,3},{24,16},{25,17},{26,18},{27,19}} | collective-permute-start | bytes 1572872 | tf_op jit(solution)/shard_map/ppermute | solution.py:19
  77.7 13.0 %collective-permute-start.11 = (bf16[256,1024]{1,0:T(8,128)(2,1)S(1)}, bf16[256,1024]{1,0:T(8,128)(2,1)S(1)}, u32[]{:S(2)}, u32[]{:S(2)}) collective-permute-start(bf16[256,1024]{1,0:T(8,128)(2,1)S(1)} %fusion.1.after.refs_0_), channel_id=1, source_target_pairs={{0,2},{1,3},{2,0},{3,1},{4,6},{5,7},{6,4},{7,5},{8,10},{9,11},{10,... | collective-permute-start | bytes 1572872 | tf_op jit(solution)/shard_map/ppermute | solution.py:19
  88.1 12.6 %collective-permute-start.15 = (bf16[512,1024]{1,0:T(8,128)(2,1)S(1)}, bf16[512,1024]{1,0:T(8,128)(2,1)S(1)}, u32[]{:S(2)}, u32[]{:S(2)}) collective-permute-start(bf16[512,1024]{1,0:T(8,128)(2,1)S(1)} %get-tuple-element.46), channel_id=1, source_target_pairs={{0,1},{1,0},{2,3},{3,2},{4,5},{5,4},{6,7},{7,6},{8,9},{9,8},{10,11... | collective-permute-start | bytes 3145736 | tf_op jit(solution)/shard_map/ppermute | solution.py:19
  88.1 4.4 %collective-permute-start.13 = (bf16[256,1024]{1,0:T(8,128)(2,1)S(1)}, bf16[256,1024]{1,0:T(8,128)(2,1)S(1)}, u32[]{:S(2)}, u32[]{:S(2)}) collective-permute-start(bf16[256,1024]{1,0:T(8,128)(2,1)S(1)} %fusion.1.after.refs_0_), channel_id=1, source_target_pairs={{0,1},{1,0},{2,3},{3,2},{4,5},{5,4},{6,7},{7,6},{8,9},{9,8},{10,11... | collective-permute-start | bytes 1572872 | tf_op jit(solution)/shard_map/ppermute | solution.py:19
  89.9 5.0 %collective-permute-start.14 = (bf16[256,1024]{1,0:T(8,128)(2,1)S(1)}, bf16[256,1024]{1,0:T(8,128)(2,1)S(1)}, u32[]{:S(2)}, u32[]{:S(2)}) collective-permute-start(bf16[256,1024]{1,0:T(8,128)(2,1)S(1)} %fusion.2.refs_0_), channel_id=1, source_target_pairs={{0,1},{1,0},{2,3},{3,2},{4,5},{5,4},{6,7},{7,6},{8,9},{9,8},{10,11... | collective-permute-start | bytes 1572872 | tf_op jit(solution)/shard_map/ppermute | solution.py:19
  90.8 6.5 %collective-permute-start.12 = (bf16[256,1024]{1,0:T(8,128)(2,1)S(1)}, bf16[256,1024]{1,0:T(8,128)(2,1)S(1)}, u32[]{:S(2)}, u32[]{:S(2)}) collective-permute-start(bf16[256,1024]{1,0:T(8,128)(2,1)S(1)} %collective-permute-done.11.refs_0_), channel_id=1, source_target_pairs={{0,1},{1,0},{2,3},{3,2},{4,5},{5,4},{6,7},{7,6},{8,9},{9,8},{10,11... | collective-permute-start | bytes 1572872 | tf_op jit(solution)/shard_map/ppermute | solution.py:19
  90.8 14.3 %collective-permute-start.10 = (bf16[256,1024]{1,0:T(8,128)(2,1)S(1)}, bf16[256,1024]{1,0:T(8,128)(2,1)S(1)}, u32[]{:S(2)}, u32[]{:S(2)}) collective-permute-start(bf16[256,1024]{1,0:T(8,128)(2,1)S(1)} %fusion.2.refs_0_), channel_id=1, source_target_pairs={{0,2},{1,3},{2,0},{3,1},{4,6},{5,7},{6,4},{7,5},{8,10},{9,11},{10,... | collective-permute-start | bytes 1572872 | tf_op jit(solution)/shard_map/ppermute | solution.py:19
  105.1 1.9 %collective-permute-start.16 = (bf16[256,1024]{1,0:T(8,128)(2,1)S(1)}, bf16[256,1024]{1,0:T(8,128)(2,1)S(1)}, u32[]{:S(2)}, u32[]{:S(2)}) collective-permute-start(bf16[256,1024]{1,0:T(8,128)(2,1)S(1)} %collective-permute-done.10.refs_0_), channel_id=1, source_target_pairs={{0,1},{1,0},{2,3},{3,2},{4,5},{5,4},{6,7},{7,6},{8,9},{9,8},{10,11... | collective-permute-start | bytes 1572872 | tf_op jit(solution)/shard_map/ppermute | solution.py:19
  (10 other events, 51.4 us)
Sparse Core Ops, SparseCore 0:
  10.2 37.1 all-gather.2

commit v2 on v1

--- a/solution.py
+++ b/solution.py
@@ -157,7 +157,7 @@
         ),
         out_shape=[jax.ShapeDtypeStruct((rows, width), F32), jax.ShapeDtypeStruct((rows, width), BF16)],
         compiler_params=params(),
-        cost_estimate=costs(0, 10 * rows * width),
+        cost_estimate=costs(8000 * rows * width, 10 * rows * width),
         name="slopes",
     )(info, stash_pre, target, after)
 
@@ -352,9 +352,7 @@
         stride *= 2
     last = [step_down(leaving[0], stride)]
     last.append(step_down(leaving[1], stride))
-    last[0], received[0], grad_w, grad_bias = lax.optimization_barrier(
-        (last[0], received[0], grad_w, grad_bias)
-    )
+    last[0], received[0], grad_w = lax.optimization_barrier((last[0], received[0], grad_w))
 
     if kept_back is not None:
         leaving[0] = kept_back
@@ -367,7 +365,7 @@
         )
         if h == 0:
             to_other, kept = terms(pre_grad, weight, info, BLOCKS, inputs[0], token)
-            last[1], to_other = lax.optimization_barrier((last[1], to_other))
+            last[1], to_other, grad_bias = lax.optimization_barrier((last[1], to_other, grad_bias))
         carries.append(carry)
     beside = kept.astype(F32) + swap_cores(to_other).astype(F32)
     far = [sum(part[h].astype(F32) for part in received) for h in range(2)]

time: 118 us -> 115 us (0.975); the launches traced: 117 us -> 115 us
  waiting for transfers between devices: 19.6 us -> 23.9 us
  local copies, waits for them, and re-layouts: 8.73 us -> 5.08 us
  starting transfers between devices: 21.6 us -> 20.4 us
    ppermute x17, waiting for transfers between devices: 19.5 us -> 23.9 us  [over(): return lax.ppermute(shard, axis, pairs)]
    unnamed x33 -> x41, local copies, waits for them, and re-layouts: 6.54 us -> 2.9 us
    ppermute x17, starting transfers between devices: 21.6 us -> 20.4 us  [over(): return lax.ppermute(shard, axis, pairs)]
    select_n x2, other arithmetic: 2.93 us -> 1.73 us  [local(): jnp.where(is_first, first_input, from_before[h * half:(h + 1) * half])]
  transfers between devices with their start and end apart: 18 -> 18, of which waited for: 7 -> 7; matrix products, arithmetic and copies ran while one was open for 19% -> 18% of each run, Pallas kernels for 24% -> 25%
where the time goes in v2:
time: 115 us
  Pallas kernels  30.8 us (27%)
  waiting for transfers between devices  23.9 us (21%)
  starting transfers between devices  20.4 us (18%)
  between operations  15.3 us (13%)
  matrix products  10.6 us (9%)
  other arithmetic  8.9 us (8%)
  local copies, waits for them, and re-layouts  5.08 us (4%)
    ppermute x17, waiting for transfers between devices, over(): return lax.ppermute(shard, axis, pairs)  23.9 us
    ppermute x17, starting transfers between devices, over(): return lax.ppermute(shard, axis, pairs)  20.4 us
    pallas_call x5, Pallas kernels, forward_step(): pl.pallas_call(functools.partial(forward_kernel, finish, count), grid_spe...  12.5 us
    dot_general x1, matrix products, local(): lax.dot_general(stashed_full, pre_grad, (((0,), (0,)), ((), ())), preferr...  10.6 us
    pallas_call x1, Pallas kernels, lookup_sum(): pl.pallas_call(lookup_kernel, grid_spec=pltpu.PrefetchScalarGridSpec(num_...  6.31 us
    pallas_call x1, Pallas kernels, first_terms(): pl.pallas_call(first_terms_kernel, grid_spec=pltpu.PrefetchScalarGridSpec...  5.34 us
    pallas_call x1, Pallas kernels, slopes(): pl.pallas_call(slopes_kernel, grid_spec=pltpu.PrefetchScalarGridSpec(num_...  3.39 us
    pallas_call x1, Pallas kernels, terms(): pl.pallas_call(terms_kernel, grid_spec=pltpu.PrefetchScalarGridSpec(num_s...  3.29 us
  transfers between devices with their start and end apart: 18, of which 7 were waited for; matrix products, arithmetic and copies ran while one was open for 18% of the time, Pallas kernels for 25%

profile of v2, /device:TPU:0, one launch (start us, length us, event | category | flops | bytes accessed | tf_op | source)
XLA Modules:
  0.0 115.0 jit_solution(7277856504095567748)
XLA Ops:
  9.8 1.3 %collective-permute-start.1 = (bf16[512,1024]{1,0:T(8,128)(2,1)}, bf16[512,1024]{1,0:T(8,128)(2,1)}, u32[]{:S(2)}, u32[]{:S(2)}) collective-permute-start(bf16[512,1024]{1,0:T(8,128)(2,1)} %bitcast.7), channel_id=1, source_target_pairs={{4,0},{8,4},{12,8},{5,1},{9,5},{13,9},{6,2},{10,6},{14,10},{7,3},{... | collective-permute-start | bytes 3145736 | tf_op jit(solution)/shard_map/ppermute | solution.py:19
  12.0 1.7 %copy-done.4 = bf16[1196,1024]{1,0:T(8,128)(2,1)S(1)} copy-done((bf16[1196,1024]{1,0:T(8,128)(2,1)S(1)}, bf16[1196,1024]{1,0:T(8,128)(2,1)}, u32[]{:S(2)}) %copy-start.4) | copy-done | bytes 2449432
  13.7 6.3 %lookup_sum.1.after = bf16[512,1024]{1,0:T(8,128)(2,1)S(1)} custom-call(s32[8]{0:T(128)S(1)} %stack.39.info.refs_5_.refs_3_, s32[64,256]{1,0:T(8,128)S(1)} %reshape.16.idx, f32[64,256]{1,0:T(8,128)S(1)} %reshape.17.amp, f32[512,2]{1,0:T(8,128)S(1)} %copy.23.fa, f32[2,1024]{1,0:T(2,128)S(1)} %copy-done.7, bf16[1196,1024]{1,0:T(8,128)(2,1)S(1)} %copy-done.4), custom_call_target="tpu_custom_call" | custom-call | flops 6270484480 | bytes 2449408 | tf_op jit(solution)/shard_map/lookup_sum/pallas_call | solution.py:99
  20.1 1.3 %collective-permute-start = (bf16[384,1024]{1,0:T(8,128)(2,1)S(1)}, bf16[384,1024]{1,0:T(8,128)(2,1)S(1)}, u32[]{:S(2)}, u32[]{:S(2)}) collective-permute-start(bf16[384,1024]{1,0:T(8,128)(2,1)S(1)} %slice.33), channel_id=1, source_target_pairs={{4,0},{12,8},{5,1},{13,9},{6,2},{14,10},{7,3},{15,11},{20,16},{28,... | collective-permute-start | bytes 2359304 | tf_op jit(solution)/shard_map/ppermute | solution.py:19
  21.4 6.0 %collective-permute-start.3 = (bf16[512,1024]{1,0:T(8,128)(2,1)S(1)}, bf16[512,1024]{1,0:T(8,128)(2,1)S(1)}, u32[]{:S(2)}, u32[]{:S(2)}) collective-permute-start(bf16[512,1024]{1,0:T(8,128)(2,1)S(1)} %bitcast.41), channel_id=1, source_target_pairs={{0,4},{4,8},{8,12},{1,5},{5,9},{9,13},{2,6},{6,10},{10,14},{3,7},{... | collective-permute-start | bytes 3145736 | tf_op jit(solution)/shard_map/ppermute | solution.py:19
  27.4 3.4 %slopes.1 = (f32[512,1024]{1,0:T(8,128)S(1)}, bf16[512,1024]{1,0:T(8,128)(2,1)S(1)}) custom-call(s32[8]{0:T(128)S(1)} %stack.39.info.refs_5_.refs_3_, bf16[1,2,512,1024]{3,2,1,0:T(8,128)(2,1)S(1)} %copy-done.5, bf16[512,1024]{1,0:T(8,128)(2,1)S(1)} %copy-done.6, bf16[512,1024]{1,0:T(8,128)(2,1)S(1)} %lookup_sum.1.after), custom_call_target="tpu_custom_call" | custom-call | flops 4194304000 | bytes 5242880 | tf_op jit(solution)/shard_map/slopes/pallas_call | solution.py:146
  30.8 8.3 %collective-permute-done.1.came = bf16[512,1024]{1,0:T(8,128)(2,1)} collective-permute-done((bf16[512,1024]{1,0:T(8,128)(2,1)}, bf16[512,1024]{1,0:T(8,128)(2,1)}, u32[]{:S(2)}, u32[]{:S(2)}) %collective-permute-start.1) | collective-permute-done | bytes 1048608 | tf_op jit(solution)/shard_map/ppermute | solution.py:19
  39.1 5.3 %gradient_terms.1 = (bf16[512,1024]{1,0:T(8,128)(2,1)S(1)}, bf16[192,1024]{1,0:T(8,128)(2,1)S(1)}, bf16[320,1024]{1,0:T(8,128)(2,1)S(1)}, bf16[192,1024]{1,0:T(8,128)(2,1)S(1)}, bf16[320,1024]{1,0:T(8,128)(2,1)S(1)}) custom-call(s32[8]{0:T(128)S(1)} %stack.39.info.refs_5_.refs_3_, bf16[512,1024]{1,0:T(8,128)(2,1)} %collective-permute-done.1.came, ...), custom_call_target="tpu_custom_call" | custom-call | flops 2147483648 | bytes 7340032 | tf_op jit(solution)/shard_map/gradient_terms/pallas_call | solution.py:185
  47.2 2.0 %collective-permute-start.7 = (bf16[192,1024]{1,0:T(8,128)(2,1)S(1)}, bf16[192,1024]{1,0:T(8,128)(2,1)}, u32[]{:S(2)}, u32[]{:S(2)}) collective-permute-start(bf16[192,1024]{1,0:T(8,128)(2,1)S(1)} %add_convert_fusion.6.later), channel_id=1, source_target_pairs={{0,2},{1,3},{2,0},{3,1},{4,6},{5,7},{6,4},{7,5},{8,10},{9,11},{10,... | collective-permute-start | bytes 1179656 | tf_op jit(solution)/shard_map/ppermute | solution.py:19
  49.2 6.6 %collective-permute-done = bf16[384,1024]{1,0:T(8,128)(2,1)S(1)} collective-permute-done((bf16[384,1024]{1,0:T(8,128)(2,1)S(1)}, bf16[384,1024]{1,0:T(8,128)(2,1)S(1)}, u32[]{:S(2)}, u32[]{:S(2)}) %collective-permute-start) | collective-permute-done | bytes 786464 | tf_op jit(solution)/shard_map/ppermute | solution.py:19
  59.4 2.0 %collective-permute-start.9 = (bf16[320,1024]{1,0:T(8,128)(2,1)}, bf16[320,1024]{1,0:T(8,128)(2,1)}, u32[]{:S(2)}, u32[]{:S(2)}) collective-permute-start(bf16[320,1024]{1,0:T(8,128)(2,1)} %add_convert_fusion.1), channel_id=1, source_target_pairs={{0,2},{1,3},{2,0},{3,1},{4,6},{5,7},{6,4},{7,5},{8,10},{9,11},{10,... | collective-permute-start | bytes 1966088 | tf_op jit(solution)/shard_map/ppermute | solution.py:19
  61.4 10.6 %convolution_convert_fusion = bf16[4096,1024]{1,0:T(8,128)(2,1)} fusion(bf16[512,1024]{1,0:T(8,128)(2,1)} %copy-done.1, bf16[1,1,512,4096]{3,2,1,0:T(8,128)(2,1)} %all-gather.3.cloned.1.call-done), kind=kOutput, calls=%fused_computation | convolution fusion | flops 4299161600 | bytes 13631488 | tf_op jit(solution)/shard_map/dot_general | solution.py:342
  73.3 1.5 %collective-permute-start.5 = (bf16[256,1024]{1,0:T(8,128)(2,1)S(1)}, bf16[256,1024]{1,0:T(8,128)(2,1)S(1)}, u32[]{:S(2)}, u32[]{:S(2)}) collective-permute-start(bf16[256,1024]{1,0:T(8,128)(2,1)S(1)} %add_convert_fusion.4), channel_id=1, source_target_pairs={{8,0},{9,1},{10,2},{11,3},{24,16},{25,17},{26,18},{27,19}} | collective-permute-start | bytes 1572872 | tf_op jit(solution)/shard_map/ppermute | solution.py:19
  74.9 1.5 %fusion.1.after.refs_0_ = bf16[256,1024]{1,0:T(8,128)(2,1)S(1)} fusion(bf16[256,1024]{1,0:T(8,128)(2,1)} %collective-permute-done.6, bf16[256,1024]{1,0:T(8,128)(2,1)} %add_convert_fusion.5, bf16[512,1024]{1,0:T(8,128)(2,1)S(1)} %copy-done.9, pred[]{:T(512)S(6)} %eq.7), kind=kLoop, calls=%fused_computation.10 | loop fusion | flops 1310720 | bytes 2097153 | tf_op jit(solution)/shard_map/jit(_where)/select_n | solution.py:362
  76.4 1.4 %collective-permute-start.11 = (bf16[256,1024]{1,0:T(8,128)(2,1)S(1)}, bf16[256,1024]{1,0:T(8,128)(2,1)S(1)}, u32[]{:S(2)}, u32[]{:S(2)}) collective-permute-start(bf16[256,1024]{1,0:T(8,128)(2,1)S(1)} %fusion.1.after.refs_0_), channel_id=1, source_target_pairs={{0,2},{1,3},{2,0},{3,1},{4,6},{5,7},{6,4},{7,5},{8,10},{9,11},{10,... | collective-permute-start | bytes 1572872 | tf_op jit(solution)/shard_map/ppermute | solution.py:19
  78.6 3.3 %input_terms.1 = (bf16[512,1024]{1,0:T(8,128)(2,1)S(1)}, bf16[512,1024]{1,0:T(8,128)(2,1)S(1)}) custom-call(s32[8]{0:T(128)S(1)} %stack.39.info.refs_5_.refs_3_, bf16[512,1024]{1,0:T(8,128)(2,1)S(1)} %copy-done.2, bf16[4096,1024]{1,0:T(8,128)(2,1)S(1)} %bitcast.28, bf16[4096,1024]{1,0:T(8,128)(2,1)S(1)} %bitcast.29, ...), custom_call_target="tpu_custom_call" | custom-call | tf_op jit(solution)/shard_map/input_terms/pallas_call | solution.py:217
  81.9 6.4 %collective-permute-done.5 = bf16[256,1024]{1,0:T(8,128)(2,1)S(1)} collective-permute-done((bf16[256,1024]{1,0:T(8,128)(2,1)S(1)}, bf16[256,1024]{1,0:T(8,128)(2,1)S(1)}, u32[]{:S(2)}, u32[]{:S(2)}) %collective-permute-start.5) | collective-permute-done | bytes 524320 | tf_op jit(solution)/shard_map/ppermute | solution.py:19
  90.4 1.4 %collective-permute-done.13.refs_1_ = bf16[256,1024]{1,0:T(8,128)(2,1)S(1)} collective-permute-done((bf16[256,1024]{1,0:T(8,128)(2,1)S(1)}, bf16[256,1024]{1,0:T(8,128)(2,1)S(1)}, u32[]{:S(2)}, u32[]{:S(2)}) %collective-permute-start.13) | collective-permute-done | bytes 524320 | tf_op jit(solution)/shard_map/ppermute | solution.py:19
  91.7 2.4 %forward_step.5.refs_4_ = f32[256,1024]{1,0:T(8,128)S(1)} custom-call(s32[8]{0:T(128)S(1)} %stack.39.info.refs_5_.refs_3_, bf16[256,1024]{1,0:T(8,128)(2,1)S(1)} %fusion.1.after.refs_0_, bf16[256,1024]{1,0:T(8,128)(2,1)S(1)} %collective-permute-done.13.refs_1_, bf16[4096,1024]{1,0:T(8,128)(2,1)S(1)} %bitcast.30, bf16[4096,1024]{1,0:T(8,128)(2,1)S(1)} %bitcast.31, ...), custom_call_target="tpu_custom_call" | custom-call | flops 1073741824 | bytes 6291456 | tf_op jit(solution)/shard_map/forward_step/pallas_call | solution.py:254
  94.1 2.4 %forward_step.6.refs_5_.refs_2_ = f32[256,1024]{1,0:T(8,128)S(1)} custom-call(s32[8]{0:T(128)S(1)} %stack.39.info.refs_5_.refs_3_, bf16[256,1024]{1,0:T(8,128)(2,1)S(1)} %fusion.2.refs_0_, bf16[256,1024]{1,0:T(8,128)(2,1)S(1)} %collective-permute-done.14.refs_1_, bf16[4096,1024]{1,0:T(8,128)(2,1)S(1)} %bitcast.32, bf16[4096,1024]{1,0:T(8,128)(2,1)S(1)} %bitcast.33, ...), custom_call_target="tpu_custom_call" | custom-call | flops 1073741824 | bytes 6291456 | tf_op jit(solution)/shard_map/forward_step/pallas_call | solution.py:254
  96.5 3.4 %forward_step.7.refs_3_ = bf16[512,1024]{1,0:T(8,128)(2,1)} custom-call(s32[8]{0:T(128)S(1)} %stack.39.info.refs_5_.refs_3_, bf16[256,1024]{1,0:T(8,128)(2,1)S(1)} %collective-permute-done.11.refs_0_, bf16[256,1024]{1,0:T(8,128)(2,1)S(1)} %collective-permute-done.12.refs_1_, bf16[4096,1024]{1,0:T(8,128)(2,1)S(1)} %bitcast.34, ...), custom_call_target="tpu_custom_call" | custom-call | flops 1073741824 | bytes 6291456 | tf_op jit(solution)/shard_map/forward_step/pallas_call | solution.py:254
  99.9 2.8 %add_convert_fusion = bf16[512,1024]{1,0:T(8,128)(2,1)} fusion(bf16[512,1024]{1,0:T(8,128)(2,1)S(1)} %collective-permute-done.15, bf16[512,1024]{1,0:T(8,128)(2,1)S(1)} %get-tuple-element.45, bf16[320,1024]{1,0:T(8,128)(2,1)} %collective-permute-done.9, bf16[192,1024]{1,0:T(8,128)(2,1)} %collective-permute-done.7), kind=kLoop, calls=%fused_computation.2 | loop fusion | flops 4718592 | bytes 4194304 | tf_op jit(solution)/shard_map/convert_element_type | solution.py:372
  103.6 1.8 %forward_step.8.refs_2_ = f32[256,1024]{1,0:T(8,128)S(1)} custom-call(s32[8]{0:T(128)S(1)} %stack.39.info.refs_5_.refs_3_, bf16[256,1024]{1,0:T(8,128)(2,1)S(1)} %collective-permute-done.10.refs_0_, bf16[4096,1024]{1,0:T(8,128)(2,1)S(1)} %bitcast.36, f32[256,1024]{1,0:T(8,128)S(1)} %forward_step.6.refs_5_.refs_2_, s32[8]{0:T(128)S(1)} %stack.39.info.refs_5_.refs_3_), custom_call_target="tpu_custom_call" | custom-call | flops 536870912 | bytes 4194304 | tf_op jit(solution)/shard_map/forward_step/pallas_call | solution.py:254
  105.5 2.6 %forward_step.9 = bf16[512,1024]{1,0:T(8,128)(2,1)} custom-call(s32[8]{0:T(128)S(1)} %stack.39.info.refs_5_.refs_3_, bf16[256,1024]{1,0:T(8,128)(2,1)S(1)} %collective-permute-done.16.refs_0_, bf16[4096,1024]{1,0:T(8,128)(2,1)S(1)} %bitcast.37, f32[256,1024]{1,0:T(8,128)S(1)} %forward_step.8.refs_2_, ...), custom_call_target="tpu_custom_call", output_to_operand_aliasing={{}: (4, {})} | custom-call | flops 536870912 | bytes 4194304 | tf_op jit(solution)/shard_map/forward_step/pallas_call | solution.py:254
  (82 shorter events, 14.2 us)
Async XLA Ops:
  7.2 54.2 %all-gather.3.cloned.1.call-start = ((), (), s32[]{:S(2)}) async-start(), calls=%async_computation | async-start | bytes 5242880 | tf_op jit(solution)/shard_map/all_gather | solution.py:310
  9.8 29.2 %collective-permute-start.1 = (bf16[512,1024]{1,0:T(8,128)(2,1)}, bf16[512,1024]{1,0:T(8,128)(2,1)}, u32[]{:S(2)}, u32[]{:S(2)}) collective-permute-start(bf16[512,1024]{1,0:T(8,128)(2,1)} %bitcast.7), channel_id=1, source_target_pairs={{4,0},{8,4},{12,8},{5,1},{9,5},{13,9},{6,2},{10,6},{14,10},{7,3},{... | collective-permute-start | bytes 3145736 | tf_op jit(solution)/shard_map/ppermute | solution.py:19
  13.7 13.7 %copy-start.6 = (bf16[512,1024]{1,0:T(8,128)(2,1)S(1)}, bf16[512,1024]{1,0:T(8,128)(2,1)}, u32[]{:S(2)}) copy-start(bf16[512,1024]{1,0:T(8,128)(2,1)} %target.1) | copy-start | bytes 3145732
  20.1 35.7 %collective-permute-start = (bf16[384,1024]{1,0:T(8,128)(2,1)S(1)}, bf16[384,1024]{1,0:T(8,128)(2,1)S(1)}, u32[]{:S(2)}, u32[]{:S(2)}) collective-permute-start(bf16[384,1024]{1,0:T(8,128)(2,1)S(1)} %slice.33), channel_id=1, source_target_pairs={{4,0},{12,8},{5,1},{13,9},{6,2},{14,10},{7,3},{15,11},{20,16},{28,... | collective-permute-start | bytes 2359304 | tf_op jit(solution)/shard_map/ppermute | solution.py:19
  21.4 17.7 %slice-start = ((s8[8388608]{0:T(1024)(128)(4,1)}), s8[4194304]{0:T(1024)(128)(4,1)S(1)}, s32[]{:S(2)}) async-start(s8[8388608]{0:T(1024)(128)(4,1)} %bitcast.22), calls=%async_computation.1 | async-start | bytes 8388608
  21.4 17.7 %slice-start.1 = ((s8[8388608]{0:T(1024)(128)(4,1)}), s8[4194304]{0:T(1024)(128)(4,1)S(1)}, s32[]{:S(2)}) async-start(s8[8388608]{0:T(1024)(128)(4,1)} %bitcast.22), calls=%async_computation.2 | async-start | bytes 8388608
  21.4 34.4 %collective-permute-start.3 = (bf16[512,1024]{1,0:T(8,128)(2,1)S(1)}, bf16[512,1024]{1,0:T(8,128)(2,1)S(1)}, u32[]{:S(2)}, u32[]{:S(2)}) collective-permute-start(bf16[512,1024]{1,0:T(8,128)(2,1)S(1)} %bitcast.41), channel_id=1, source_target_pairs={{0,4},{4,8},{8,12},{1,5},{5,9},{9,13},{2,6},{6,10},{10,14},{3,7},{... | collective-permute-start | bytes 3145736 | tf_op jit(solution)/shard_map/ppermute | solution.py:19
  44.4 14.9 %copy-start.1 = (bf16[512,1024]{1,0:T(8,128)(2,1)}, bf16[512,1024]{1,0:T(8,128)(2,1)S(1)}, u32[]{:S(2)}) copy-start(bf16[512,1024]{1,0:T(8,128)(2,1)S(1)} %get-tuple-element.34.grad) | copy-start | bytes 3145732
  44.4 2.6 %collective-permute-start.2 = (bf16[192,1024]{1,0:T(8,128)(2,1)S(1)}, bf16[192,1024]{1,0:T(8,128)(2,1)S(1)}, u32[]{:S(2)}, u32[]{:S(2)}) collective-permute-start(bf16[192,1024]{1,0:T(8,128)(2,1)S(1)} %get-tuple-element.32), channel_id=1, source_target_pairs={{0,1},{1,0},{2,3},{3,2},{4,5},{5,4},{6,7},{7,6},{8,9},{9,8},{10,11... | collective-permute-start | bytes 1179656 | tf_op jit(solution)/shard_map/ppermute | solution.py:19
  44.5 13.7 %collective-permute-start.8 = (bf16[320,1024]{1,0:T(8,128)(2,1)S(1)}, bf16[320,1024]{1,0:T(8,128)(2,1)S(1)}, u32[]{:S(2)}, u32[]{:S(2)}) collective-permute-start(bf16[320,1024]{1,0:T(8,128)(2,1)S(1)} %get-tuple-element.38), channel_id=1, source_target_pairs={{0,1},{1,0},{2,3},{3,2},{4,5},{5,4},{6,7},{7,6},{8,9},{9,8},{10,11... | collective-permute-start | bytes 1966088 | tf_op jit(solution)/shard_map/ppermute | solution.py:19
  45.7 26.3 %collective-permute-start.4 = (bf16[128,1024]{1,0:T(8,128)(2,1)}, bf16[128,1024]{1,0:T(8,128)(2,1)}, u32[]{:S(2)}, u32[]{:S(2)}) collective-permute-start(bf16[128,1024]{1,0:T(8,128)(2,1)} %slice.34), channel_id=1, source_target_pairs={{4,0},{12,8},{5,1},{13,9},{6,2},{14,10},{7,3},{15,11},{20,16},{28,... | collective-permute-start | bytes 786440 | tf_op jit(solution)/shard_map/ppermute | solution.py:19
  47.2 27.6 %collective-permute-start.7 = (bf16[192,1024]{1,0:T(8,128)(2,1)S(1)}, bf16[192,1024]{1,0:T(8,128)(2,1)}, u32[]{:S(2)}, u32[]{:S(2)}) collective-permute-start(bf16[192,1024]{1,0:T(8,128)(2,1)S(1)} %add_convert_fusion.6.later), channel_id=1, source_target_pairs={{0,2},{1,3},{2,0},{3,1},{4,6},{5,7},{6,4},{7,5},{8,10},{9,11},{10,... | collective-permute-start | bytes 1179656 | tf_op jit(solution)/shard_map/ppermute | solution.py:19
  57.0 17.8 %collective-permute-start.6 = (bf16[256,1024]{1,0:T(8,128)(2,1)}, bf16[256,1024]{1,0:T(8,128)(2,1)}, u32[]{:S(2)}, u32[]{:S(2)}) collective-permute-start(bf16[256,1024]{1,0:T(8,128)(2,1)} %add_convert_fusion.5), channel_id=1, source_target_pairs={{8,0},{9,1},{10,2},{11,3},{24,16},{25,17},{26,18},{27,19}} | collective-permute-start | bytes 1572872 | tf_op jit(solution)/shard_map/ppermute | solution.py:19
  59.4 15.6 %collective-permute-start.9 = (bf16[320,1024]{1,0:T(8,128)(2,1)}, bf16[320,1024]{1,0:T(8,128)(2,1)}, u32[]{:S(2)}, u32[]{:S(2)}) collective-permute-start(bf16[320,1024]{1,0:T(8,128)(2,1)} %add_convert_fusion.1), channel_id=1, source_target_pairs={{0,2},{1,3},{2,0},{3,1},{4,6},{5,7},{6,4},{7,5},{8,10},{9,11},{10,... | collective-permute-start | bytes 1966088 | tf_op jit(solution)/shard_map/ppermute | solution.py:19
  61.4 17.2 %slice-start.2 = ((s8[8388608]{0:T(1024)(128)(4,1)}), s8[4194304]{0:T(1024)(128)(4,1)S(1)}, s32[]{:S(2)}) async-start(s8[8388608]{0:T(1024)(128)(4,1)} %bitcast.26), calls=%async_computation.3 | async-start | bytes 8388608
  61.4 17.2 %slice-start.3 = ((s8[8388608]{0:T(1024)(128)(4,1)}), s8[4194304]{0:T(1024)(128)(4,1)S(1)}, s32[]{:S(2)}) async-start(s8[8388608]{0:T(1024)(128)(4,1)} %bitcast.26), calls=%async_computation.4 | async-start | bytes 8388608
  73.3 15.0 %collective-permute-start.5 = (bf16[256,1024]{1,0:T(8,128)(2,1)S(1)}, bf16[256,1024]{1,0:T(8,128)(2,1)S(1)}, u32[]{:S(2)}, u32[]{:S(2)}) collective-permute-start(bf16[256,1024]{1,0:T(8,128)(2,1)S(1)} %add_convert_fusion.4), channel_id=1, source_target_pairs={{8,0},{9,1},{10,2},{11,3},{24,16},{25,17},{26,18},{27,19}} | collective-permute-start | bytes 1572872 | tf_op jit(solution)/shard_map/ppermute | solution.py:19
  76.4 12.8 %collective-permute-start.11 = (bf16[256,1024]{1,0:T(8,128)(2,1)S(1)}, bf16[256,1024]{1,0:T(8,128)(2,1)S(1)}, u32[]{:S(2)}, u32[]{:S(2)}) collective-permute-start(bf16[256,1024]{1,0:T(8,128)(2,1)S(1)} %fusion.1.after.refs_0_), channel_id=1, source_target_pairs={{0,2},{1,3},{2,0},{3,1},{4,6},{5,7},{6,4},{7,5},{8,10},{9,11},{10,... | collective-permute-start | bytes 1572872 | tf_op jit(solution)/shard_map/ppermute | solution.py:19
  88.3 11.6 %collective-permute-start.15 = (bf16[512,1024]{1,0:T(8,128)(2,1)S(1)}, bf16[512,1024]{1,0:T(8,128)(2,1)S(1)}, u32[]{:S(2)}, u32[]{:S(2)}) collective-permute-start(bf16[512,1024]{1,0:T(8,128)(2,1)S(1)} %get-tuple-element.46), channel_id=1, source_target_pairs={{0,1},{1,0},{2,3},{3,2},{4,5},{5,4},{6,7},{7,6},{8,9},{9,8},{10,11... | collective-permute-start | bytes 3145736 | tf_op jit(solution)/shard_map/ppermute | solution.py:19
  88.3 3.4 %collective-permute-start.13 = (bf16[256,1024]{1,0:T(8,128)(2,1)S(1)}, bf16[256,1024]{1,0:T(8,128)(2,1)S(1)}, u32[]{:S(2)}, u32[]{:S(2)}) collective-permute-start(bf16[256,1024]{1,0:T(8,128)(2,1)S(1)} %fusion.1.after.refs_0_), channel_id=1, source_target_pairs={{0,1},{1,0},{2,3},{3,2},{4,5},{5,4},{6,7},{7,6},{8,9},{9,8},{10,11... | collective-permute-start | bytes 1572872 | tf_op jit(solution)/shard_map/ppermute | solution.py:19
  89.1 5.0 %collective-permute-start.14 = (bf16[256,1024]{1,0:T(8,128)(2,1)S(1)}, bf16[256,1024]{1,0:T(8,128)(2,1)S(1)}, u32[]{:S(2)}, u32[]{:S(2)}) collective-permute-start(bf16[256,1024]{1,0:T(8,128)(2,1)S(1)} %fusion.2.refs_0_), channel_id=1, source_target_pairs={{0,1},{1,0},{2,3},{3,2},{4,5},{5,4},{6,7},{7,6},{8,9},{9,8},{10,11... | collective-permute-start | bytes 1572872 | tf_op jit(solution)/shard_map/ppermute | solution.py:19
  89.2 7.3 %collective-permute-start.12 = (bf16[256,1024]{1,0:T(8,128)(2,1)S(1)}, bf16[256,1024]{1,0:T(8,128)(2,1)S(1)}, u32[]{:S(2)}, u32[]{:S(2)}) collective-permute-start(bf16[256,1024]{1,0:T(8,128)(2,1)S(1)} %collective-permute-done.11.refs_0_), channel_id=1, source_target_pairs={{0,1},{1,0},{2,3},{3,2},{4,5},{5,4},{6,7},{7,6},{8,9},{9,8},{10,11... | collective-permute-start | bytes 1572872 | tf_op jit(solution)/shard_map/ppermute | solution.py:19
  89.7 13.9 %collective-permute-start.10 = (bf16[256,1024]{1,0:T(8,128)(2,1)S(1)}, bf16[256,1024]{1,0:T(8,128)(2,1)S(1)}, u32[]{:S(2)}, u32[]{:S(2)}) collective-permute-start(bf16[256,1024]{1,0:T(8,128)(2,1)S(1)} %fusion.2.refs_0_), channel_id=1, source_target_pairs={{0,2},{1,3},{2,0},{3,1},{4,6},{5,7},{6,4},{7,5},{8,10},{9,11},{10,... | collective-permute-start | bytes 1572872 | tf_op jit(solution)/shard_map/ppermute | solution.py:19
  103.6 1.9 %collective-permute-start.16 = (bf16[256,1024]{1,0:T(8,128)(2,1)S(1)}, bf16[256,1024]{1,0:T(8,128)(2,1)S(1)}, u32[]{:S(2)}, u32[]{:S(2)}) collective-permute-start(bf16[256,1024]{1,0:T(8,128)(2,1)S(1)} %collective-permute-done.10.refs_0_), channel_id=1, source_target_pairs={{0,1},{1,0},{2,3},{3,2},{4,5},{5,4},{6,7},{7,6},{8,9},{9,8},{10,11... | collective-permute-start | bytes 1572872 | tf_op jit(solution)/shard_map/ppermute | solution.py:19
  (14 other events, 86.1 us)
Sparse Core Ops, SparseCore 0:
  10.2 37.2 all-gather.2
